TPU v7x, 32 devices: a whole 2x2x4 slice. The times are simulated.
32 devices in a mesh: seq: 4 (over y, x), batch: 8 (over z, core).
Axes of the slice: x: 2, y: 2, z: 4, core: 2. Of those that a mesh axis runs over, the one named last changes fastest.
Arguments:
- tokens: bfloat16 [2, 32, 1024, 1280], P(None, 'batch', 'seq'), may hold values from -8 to 8
- lengths: int32 [2, 32], P(None, 'batch'), may hold values from 30 to 1024, as said below
- first_gain: bfloat16 [1280], P('batch'), may hold values from 0.5 to 1.5
- first_shift: bfloat16 [1280], P('batch'), may hold values from -1.25 to 1.25
- down_weight: bfloat16 [1280, 640], P('seq', 'batch'), may hold values from -0.15625 to 0.15625
- down_bias: bfloat16 [640], P('batch'), may hold values from -1.25 to 1.25
- middle_gain: bfloat16 [640], P('batch'), may hold values from 0.5 to 1.5
- middle_shift: bfloat16 [640], P('batch'), may hold values from -1.25 to 1.25
- conv_weight: bfloat16 [5, 640, 640], P(None, 'seq', 'batch'), may hold values from -0.109375 to 0.109375
- conv_bias: bfloat16 [640], P('batch'), may hold values from -1.25 to 1.25
- final_gain: bfloat16 [640], P('batch'), may hold values from 0.5 to 1.5
- final_shift: bfloat16 [640], P('batch'), may hold values from -1.25 to 1.25
- up_weight: bfloat16 [640, 1280], P('seq', 'batch'), may hold values from -0.25 to 0.25
- up_bias: bfloat16 [1280], P('batch'), may hold values from -1.25 to 1.25
- cotangent: bfloat16 [2, 32, 1024, 1280], P(None, 'batch', 'seq'), may hold values from -8 to 8
Outputs:
- block_output: bfloat16 [2, 32, 1024, 1280], P(None, 'batch', 'seq')
- tokens_grad: bfloat16 [2, 32, 1024, 1280], P(None, 'batch', 'seq')
- first_gain_grad: float32 [1280], P('batch')
- first_shift_grad: float32 [1280], P('batch')
- down_weight_grad: float32 [1280, 640], P('seq', 'batch')
- down_bias_grad: float32 [640], P('batch')
- middle_gain_grad: float32 [640], P('batch')
- middle_shift_grad: float32 [640], P('batch')
- conv_weight_grad: float32 [5, 640, 640], P(None, 'seq', 'batch')
- conv_bias_grad: float32 [640], P('batch')
- final_gain_grad: float32 [640], P('batch')
- final_shift_grad: float32 [640], P('batch')
- up_weight_grad: float32 [640, 1280], P('seq', 'batch')
- up_bias_grad: float32 [1280], P('batch')
Inputs may be any that keep to these rules, and one draw needn't show every extreme that they name: `lengths`: short proteins are more common than long ones. In every micro-batch, among proteins 4 * i to 4 * (i + 1) - 1 for each i, exactly one, at a place drawn from the seed, has length 1024.
All inputs are finite; a program needn't handle non-finite values.
Results may differ from a plain program's by a relative error of at most 0.0072.
Values may be sent and summed in bfloat16 or wider, within the bound.
No kernel may reach another device: no remote copies, remote signals or barrier semaphores. Data moves between devices by JAX's collectives and lax.ppermute only.
A program may use at most 192 MiB of HBM per device.

v0:
```python
import functools
import math

import jax
import jax.numpy as jnp
from jax import lax
from jax.experimental import pallas as pl
from jax.experimental.pallas import tpu as pltpu
from jax.sharding import PartitionSpec as P

DILATION = 16
EPSILON = 1e-05
BF = jnp.bfloat16
F32 = jnp.float32
ROOT_HALF = math.sqrt(0.5)
SLOPE = 2.0 / math.sqrt(math.pi)
LOG = -math.log2(math.e)
MIB = 1 << 20
GROUP = 2
LIM2P = 60
LIM2 = 60
LIM3P = 56
LIM3 = 40
LIM4 = 48

WIDE = ("first_gain", "first_shift", "up_bias")
NARROW = ("down_bias", "middle_gain", "middle_shift", "conv_bias", "final_gain", "final_shift")
WIDE_ROWS = 3
ROW = {name: row for row, name in enumerate(WIDE + NARROW)}
TABLE_ROWS = 16


def add_up(terms, kind):
    total = terms[0].astype(F32)
    for term in terms[1:]:
        total = total + term.astype(F32)
    return total.astype(kind)


class Grid:
    def __init__(self, seq, batch):
        self.seq, self.batch = seq, batch
        self.side = math.isqrt(seq)
        assert self.side * self.side == seq
        self.depth = batch // 2
        self.half = self.depth // 2

    def here(self):
        s, b = lax.axis_index("seq"), lax.axis_index("batch")
        return s // self.side, s % self.side, b // 2, b % 2

    def send(self, value, move):
        pairs = []
        for s in range(self.seq):
            for b in range(self.batch):
                h, l, z, c = move(s // self.side, s % self.side, b // 2, b % 2)
                pairs.append((s * self.batch + b, (h * self.side + l) * self.batch + z * 2 + c))
        return lax.ppermute(value, ("seq", "batch"), pairs)

    def high(self, value, k):
        return self.send(value, lambda h, l, z, c: ((h + k) % self.side, l, z, c))

    def low(self, value, k):
        return self.send(value, lambda h, l, z, c: (h, (l + k) % self.side, z, c))

    def deep(self, value, k):
        return self.send(value, lambda h, l, z, c: (h, l, (z + k) % self.depth, c))

    def core(self, value):
        return self.send(value, lambda h, l, z, c: (h, l, z, 1 - c))

    def gather_deep(self, piece):
        return [piece] + [self.deep(piece, k) for k in range(1, self.depth)]

    def halves(self, column):
        return jnp.stack(column[: self.half]), jnp.stack(column[self.half :])

    def gather_near(self, one, two):
        one = jnp.stack([one] + [self.low(one, k) for k in range(1, self.side)])
        two = jnp.stack([two] + [self.high(two, k) for k in range(1, self.side)])
        return one, two

    def gather_far(self, one, two):
        return (
            [self.high(one, k) for k in range(1, self.side)],
            [self.low(two, k) for k in range(1, self.side)],
        )

    def gather_core(self, values):
        return [self.core(value) for value in values]

    def reduce_core(self, keep_one, keep_two, give_one, give_two):
        return (
            add_up([keep_one, self.core(give_one)], BF),
            add_up([keep_two, self.core(give_two)], BF),
        )

    def reduce_far(self, one, two):
        one = add_up([one[0]] + [self.high(one[k], -k) for k in range(1, self.side)], BF)
        two = add_up([two[0]] + [self.low(two[k], -k) for k in range(1, self.side)], BF)
        return one, two

    def reduce_near(self, one, two):
        one = add_up([one[0]] + [self.low(one[k], -k) for k in range(1, self.side)], BF)
        two = add_up([two[0]] + [self.high(two[k], -k) for k in range(1, self.side)], BF)
        return one, two

    def reduce_deep(self, one, two):
        column = [one[k] for k in range(self.half)] + [two[k] for k in range(self.half)]
        return (column[0],) + tuple(self.deep(column[k], -k) for k in range(1, self.depth))


def near_distance(grid, place, s):
    side = grid.side
    return (
        lax.rem(place[0] - s // side + side, side),
        lax.rem(place[1] - s % side + side, side),
    )


def deep_distance(grid, place, b):
    return lax.rem(place[2] - b // 2 + grid.depth, grid.depth)


def spot_of(grid, place, s, b):
    rh, rl = near_distance(grid, place, s)
    rz = deep_distance(grid, place, b)
    second = rz >= grid.half
    return (
        jnp.where(second, 1, 0),
        jnp.where(second, rl, rh),
        jnp.where(second, rh, rl),
        jnp.where(second, rz - grid.half, rz),
    )


def distance(grid, place, s, b):
    return (jnp.where(place[3] == b % 2, 0, 1),) + spot_of(grid, place, s, b)


class Order:
    def __init__(self, grid, hidden):
        self.grid, self.hidden = grid, hidden
        self.hl, self.hb = hidden // grid.seq, hidden // grid.batch
        self.main = self.hl // 128 * 128
        self.rest = self.hl - self.main

    def runs(self, first, count):
        found = []
        at = first
        while at < first + count:
            block, r = at // self.hl, at % self.hl
            if r < self.main:
                length = min(self.main - r, first + count - at)
                place = block * self.main + r
            else:
                length = min(self.hl - r, first + count - at)
                place = self.grid.seq * self.main + block * self.rest + r - self.main
            if found and found[-1][1] + found[-1][2] == place:
                found[-1] = (found[-1][0], found[-1][1], found[-1][2] + length)
            else:
                found.append((at - first, place, length))
            at += length
        return found


def join(parts):
    return parts[0] if len(parts) == 1 else jnp.concatenate(parts, axis=1)


def wire_from_rows(order, row_blocks):
    main, rest, seq = order.main, order.rest, order.grid.seq
    pieces = []
    for s in range(seq):
        parts = [block[:, s * main : (s + 1) * main] for block in row_blocks if main]
        if rest:
            at = seq * main + s * rest
            parts += [block[:, at : at + rest] for block in row_blocks]
        pieces.append(join(parts))
    return pieces


def rows_from_wire(order, pieces, count, j):
    main, rest = order.main, order.rest
    parts = [piece[:, j * main : (j + 1) * main] for piece in pieces if main]
    if rest:
        at = count * main + j * rest
        parts += [piece[:, at : at + rest] for piece in pieces]
    return join(parts)


def stage_copies(place, side, parts, stage, sems):
    copies = []
    for index, part in enumerate(parts):
        mine = index < 2 * side
        core = place[3] if mine else 1 - place[3]
        half, far = index // side % 2, index % side
        copies.append(pltpu.make_async_copy(part, stage.at[core, half, far], sems.at[index]))
    for copy in copies:
        copy.start()
    return copies


def staged(grid, place, stage, s, b):
    return stage[(b % 2,) + spot_of(grid, place, s, b)]


def hand_out(pieces, parts, sems):
    copies = [
        pltpu.make_async_copy(pieces.at[index // 2, index % 2], part, sems.at[index])
        for index, part in enumerate(parts)
    ]
    for copy in copies:
        copy.start()
    for copy in copies:
        copy.wait()


def piece_shape(grid, rows, lanes):
    return (grid.side, grid.side, grid.half, rows, lanes)


def normed(values):
    center = values - jnp.mean(values, axis=-1, keepdims=True)
    spread = jnp.mean(center * center, axis=-1, keepdims=True)
    inverse = lax.rsqrt(spread + EPSILON)
    return center * inverse, inverse


def scaled(unit, gain, shift):
    return unit * (gain * ROOT_HALF) + shift * ROOT_HALF


def gelu(x):
    return (x * ROOT_HALF) * (1.0 + lax.erf(x))


def gelu_both(x):
    twice = 1.0 + lax.erf(x)
    return (x * ROOT_HALF) * twice, twice + (x * SLOPE) * jnp.exp2((x * LOG) * x)


def back_rows(twice_q, gain, unit, inverse):
    share = 1.0 / unit.shape[-1]
    half = gain * 0.5
    product = twice_q * unit
    weighted = twice_q * half
    first = jnp.sum(weighted, axis=-1, keepdims=True) * share
    second = jnp.sum(product * half, axis=-1, keepdims=True) * share
    return (weighted - first - unit * second) * inverse, product


def row_sum(values):
    return jnp.sum(values, axis=0, keepdims=True)


def dot_nn(left, right):
    return lax.dot_general(left, right, (((1,), (0,)), ((), ())), preferred_element_type=F32)


def dot_nt(left, right):
    return lax.dot_general(left, right, (((1,), (1,)), ((), ())), preferred_element_type=F32)


def dot_tn(left, right):
    return lax.dot_general(left, right, (((0,), (0,)), ((), ())), preferred_element_type=F32)


def group_of(count):
    return GROUP if count % GROUP == 0 else 1


def valid_rows(start_ref, length_ref, group, span):
    position = start_ref[0] + lax.broadcasted_iota(jnp.int32, (span, 1), 0)
    first = pl.program_id(0) * group
    return jnp.concatenate(
        [(position < length_ref[first + g]).astype(F32) for g in range(group)], axis=0
    )


def params(limit):
    return pltpu.CompilerParams(
        dimension_semantics=("arbitrary",), vmem_limit_bytes=limit * MIB
    )


def cost(flops, bytes_accessed, transcendentals=0):
    return pl.CostEstimate(
        flops=flops, bytes_accessed=bytes_accessed, transcendentals=transcendentals
    )


def whole(shape):
    return pl.BlockSpec(shape, lambda i, *_: (0,) * len(shape))


def rows_of(block):
    return pl.BlockSpec(block, lambda i, *_: (i,) + (0,) * (len(block) - 1))


def sds(shape, kind):
    return jax.ShapeDtypeStruct(shape, kind)


def pack_first_kernel(order, down, *refs):
    values, first = refs[:-1], refs[-1]
    hb, dl = down.shape
    first[0:hb] = down[...]
    sub = lax.broadcasted_iota(jnp.int32, (16, dl), 0)
    tail = jnp.zeros((16, dl), F32)
    for row, ref in enumerate(values):
        value = ref[...].astype(F32).reshape(1, -1)
        if value.shape[1] < dl:
            value = join([value, jnp.zeros((1, dl - value.shape[1]), F32)])
        tail = tail + jnp.where(sub == row, value, 0.0)
    first[hb : hb + 16] = tail.astype(BF)


def pack_first(order, down, values):
    hb, dl = down.shape
    return pl.pallas_call(
        functools.partial(pack_first_kernel, order),
        out_shape=sds((hb + 16, dl), BF),
        grid=(1,),
        in_specs=[whole(down.shape)] + [whole(value.shape) for value in values],
        out_specs=whole((hb + 16, dl)),
        compiler_params=params(60),
        cost_estimate=cost(0, 4 * hb * dl),
        name="pack_first",
    )(down, *values)


def pack_second_kernel(order, conv, up, second):
    hb, taps = order.hb, conv.shape[0]
    fold = up.shape[1] // hb
    blocks = [conv[k].astype(F32).T.astype(BF) for k in range(taps)]
    turned = up[...].astype(F32).T.astype(BF)
    blocks += [turned[f * hb : (f + 1) * hb] for f in range(fold)]
    parts = [block[:, : order.main] for block in blocks if order.main]
    if order.rest:
        parts += [block[:, order.main :] for block in blocks]
    second[...] = join(parts)


def pack_second(order, conv, up):
    hb = order.hb
    blocks = conv.shape[0] + up.shape[1] // hb
    return pl.pallas_call(
        functools.partial(pack_second_kernel, order),
        out_shape=sds((hb, blocks * order.hl), BF),
        grid=(1,),
        in_specs=[whole(conv.shape), whole(up.shape)],
        out_specs=whole((hb, blocks * order.hl)),
        compiler_params=params(60),
        cost_estimate=cost(0, 4 * hb * blocks * order.hl),
        name="pack_second",
    )(conv, up)


def unpack_rest_kernel(order, taps, *refs):
    terms, (conv, up) = refs[:-2], refs[-2:]
    hb = order.hb
    fold = up.shape[1] // hb
    total = add_up([term[...] for term in terms], F32)
    for j in range(taps + fold):
        block = rows_from_wire(order, [total], taps + fold, j).T
        if j < taps:
            conv[j] = block
        else:
            up[:, (j - taps) * hb : (j - taps + 1) * hb] = block


def unpack_rest(order, taps, fold, terms):
    return pl.pallas_call(
        functools.partial(unpack_rest_kernel, order, taps),
        out_shape=(
            sds((taps, order.hl, order.hb), F32),
            sds((order.hl, fold * order.hb), F32),
        ),
        compiler_params=pltpu.CompilerParams(vmem_limit_bytes=16 * MIB),
        cost_estimate=cost(0, 8 * (taps + fold) * order.hl * order.hb),
        name="unpack_rest",
    )(*terms)


def unpack_first_kernel(order, *refs):
    terms, (down, tail) = refs[:-2], refs[-2:]
    hb = order.hb
    total = add_up([term[...] for term in terms], F32)
    down[...] = total[0:hb]
    tail[...] = total[hb : hb + 16]


def unpack_first(order, terms):
    dl = terms[0].shape[1]
    return pl.pallas_call(
        functools.partial(unpack_first_kernel, order),
        out_shape=(sds((order.hb, dl), F32), sds((16, dl), F32)),
        compiler_params=pltpu.CompilerParams(vmem_limit_bytes=16 * MIB),
        cost_estimate=cost(0, 8 * dl * order.hb),
        name="unpack_first",
    )(*terms)


def stage_one_kernel(
    grid, order, place, start_ref, length_ref, tokens, *refs
):
    parts, refs = refs[: 4 * grid.side], refs[4 * grid.side :]
    hidden_one, narrow, conv_input, down_t, table, stage, sems = refs
    model = tokens.shape[2]
    hidden = narrow.shape[2]
    hb, dl = order.hb, model // grid.seq

    @pl.when(pl.program_id(0) == 0)
    def _():
        copies = stage_copies(place, grid.side, parts, stage, sems)
        for copy in copies:
            copy.wait()
        table[...] = jnp.zeros_like(table)
        for b in range(grid.batch):
            pieces = [staged(grid, place, stage, s, b) for s in range(grid.seq)]
            block = join([piece[0:hb] for piece in pieces])
            for offset, spot, length in order.runs(b * hb, hb):
                down_t[spot : spot + length] = block[offset : offset + length]
            tail = pieces[0][hb : hb + 16].astype(F32)
            wide = model // grid.batch
            table[0:WIDE_ROWS, b * wide : (b + 1) * wide] = tail[0:WIDE_ROWS, 0:wide]
            for offset, spot, length in order.runs(b * hb, hb):
                table[WIDE_ROWS:TABLE_ROWS, spot : spot + length] = tail[
                    WIDE_ROWS:TABLE_ROWS, offset : offset + length
                ]

    def vec(name, width):
        return table[ROW[name] : ROW[name] + 1, 0:width]

    group, span = tokens.shape[0], tokens.shape[1]
    unit, _ = normed(tokens[...].reshape(group * span, model).astype(F32))
    one = gelu(scaled(unit, vec("first_gain", model), vec("first_shift", model))).astype(BF)
    hidden_one[...] = one.reshape(group, span, model)
    values = dot_nt(one, down_t[...]) + vec("down_bias", hidden)
    narrow[...] = values.reshape(group, span, hidden)
    unit, _ = normed(values)
    active = gelu(scaled(unit, vec("middle_gain", hidden), vec("middle_shift", hidden)))
    valid = valid_rows(start_ref, length_ref, group, span)
    conv_input[...] = (active * valid).astype(BF).reshape(group, span, hidden)


def stage_one(grid, order, place, start, lengths, tokens, parts):
    count, span, model = tokens.shape
    hidden = order.hidden
    group = group_of(count)
    rows, lanes = parts[0].shape[-2:]
    return pl.pallas_call(
        functools.partial(stage_one_kernel, grid, order),
        out_shape=(
            sds((count, span, model), BF),
            sds((count, span, hidden), F32),
            sds((count, span, hidden), BF),
            sds((hidden, model), BF),
            sds((TABLE_ROWS, model), F32),
        ),
        grid_spec=pltpu.PrefetchScalarGridSpec(
            num_scalar_prefetch=3,
            grid=(count // group,),
            in_specs=[rows_of((group, span, model))]
            + [pl.BlockSpec(memory_space=pl.ANY)] * len(parts),
            out_specs=[
                rows_of((group, span, model)),
                rows_of((group, span, hidden)),
                rows_of((group, span, hidden)),
                whole((hidden, model)),
                whole((TABLE_ROWS, model)),
            ],
            scratch_shapes=[
                pltpu.VMEM((2, 2) + piece_shape(grid, rows, lanes), BF),
                pltpu.SemaphoreType.DMA((len(parts),)),
            ],
        ),
        compiler_params=params(54),
        cost_estimate=cost(
            2 * count * span * model * hidden, count * span * (4 * model + 6 * hidden)
        ),
        name="stage_one",
    )(place, start, lengths, tokens, *parts)


def fill_padded(padded, left, body, right):
    reach = left.shape[0]
    span = body.shape[0]
    padded[0:reach] = left
    padded[reach : reach + span] = body
    padded[reach + span : 2 * reach + span] = right


def tap_windows(padded, taps, span):
    group, _, hidden = padded.shape
    return [
        padded[:, k * DILATION : k * DILATION + span].reshape(group * span, hidden) for k in taps
    ]


def edge_windows(left, right, taps):
    count, reach, hidden = left.shape
    zeros = jnp.zeros((count, reach, hidden), BF)
    before = jnp.concatenate([left, zeros], axis=1)
    after_run = jnp.concatenate([zeros, right], axis=1)
    middle = taps // 2

    def window(rows, at):
        return rows[:, at : at + reach].reshape(count * reach, hidden)

    return (
        [window(before, k * DILATION) for k in range(middle)],
        [window(after_run, (k - middle) * DILATION) for k in range(middle + 1, taps)],
    )


def add_edges(part, edges):
    group, span, hidden = part.shape
    reach = edges.shape[1] // 2
    rows = [part[:, 0:reach] + edges[:, 0:reach]]
    if span > 2 * reach:
        rows.append(part[:, reach : span - reach])
    rows.append(part[:, span - reach : span] + edges[:, reach : 2 * reach])
    return jnp.concatenate(rows, axis=1).reshape(group * span, hidden)


def inner_kernel(
    grid, order, taps, place, cotangent, conv_input, *refs
):
    parts, refs = refs[: 4 * grid.side], refs[4 * grid.side :]
    part, error, conv_t, up_out, conv_f, up_t, padded, stage, sems, out_sems = refs
    group, span, model = cotangent.shape
    hidden = conv_input.shape[2]
    reach = (padded.shape[1] - span) // 2
    hb = order.hb
    fold = model // hidden

    def weight_copies():
        return [
            pltpu.make_async_copy(
                conv_f.at[:, k * hidden : (k + 1) * hidden], conv_t.at[k], out_sems.at[k]
            )
            for k in range(taps)
        ] + [pltpu.make_async_copy(up_t, up_out, out_sems.at[taps])]

    @pl.when(pl.program_id(0) == 0)
    def _():
        copies = stage_copies(place, grid.side, parts, stage, sems)
        padded[:, 0:reach] = jnp.zeros((group, reach, hidden), BF)
        padded[:, reach + span : 2 * reach + span] = jnp.zeros((group, reach, hidden), BF)
        for copy in copies:
            copy.wait()
        for b in range(grid.batch):
            wires = [staged(grid, place, stage, s, b) for s in range(grid.seq)]
            for k in range(taps):
                block = rows_from_wire(order, wires, taps + fold, k)
                for offset, spot, length in order.runs(b * hb, hb):
                    conv_f[spot : spot + length, k * hidden : (k + 1) * hidden] = block[
                        offset : offset + length
                    ]
            for f in range(fold):
                row = (b * fold + f) * hb
                up_t[row : row + hb] = rows_from_wire(order, wires, taps + fold, taps + f)
        for copy in weight_copies():
            copy.start()

    padded[:, reach : reach + span] = conv_input[...]
    windows = join(tap_windows(padded, range(taps), span))
    part[...] = dot_nt(windows, conv_f[...]).reshape(group, span, hidden)
    incoming = cotangent[...].reshape(group * span, model)
    error[...] = dot_nn(incoming, up_t[...]).reshape(group, span, hidden)

    @pl.when(pl.program_id(0) == pl.num_programs(0) - 1)
    def _():
        for copy in weight_copies():
            copy.wait()


def inner(grid, order, taps, reach, place, cotangent, conv_input, parts):
    count, span, model = cotangent.shape
    hidden = order.hidden
    group = group_of(count)
    rows, lanes = parts[0].shape[-2:]
    return pl.pallas_call(
        functools.partial(inner_kernel, grid, order, taps),
        out_shape=(
            sds((count, span, hidden), F32),
            sds((count, span, hidden), F32),
            sds((taps, hidden, hidden), BF),
            sds((model, hidden), BF),
        ),
        grid_spec=pltpu.PrefetchScalarGridSpec(
            num_scalar_prefetch=1,
            grid=(count // group,),
            in_specs=[rows_of((group, span, model)), rows_of((group, span, hidden))]
            + [pl.BlockSpec(memory_space=pl.ANY)] * len(parts),
            out_specs=[
                rows_of((group, span, hidden)),
                rows_of((group, span, hidden)),
                pl.BlockSpec(memory_space=pl.ANY),
                pl.BlockSpec(memory_space=pl.ANY),
            ],
            scratch_shapes=[
                pltpu.VMEM((hidden, taps * hidden), BF),
                pltpu.VMEM((model, hidden), BF),
                pltpu.VMEM((group, span + 2 * reach, hidden), BF),
                pltpu.VMEM((2, 2) + piece_shape(grid, rows, lanes), BF),
                pltpu.SemaphoreType.DMA((len(parts),)),
                pltpu.SemaphoreType.DMA((taps + 1,)),
            ],
        ),
        compiler_params=params(LIM2P),
        cost_estimate=cost(
            2 * count * span * hidden * (taps * hidden + model),
            count * span * (2 * model + 10 * hidden),
        ),
        name="inner",
    )(place, cotangent, conv_input, *parts)


def stage_two_kernel(
    grid, order, taps, place, tokens, cotangent, conv_input, left, right, part, error, table,
    conv_t, up_t,
    output, conv_out_grad, sums, part_a, part_b, part_c, part_d,
    padded, threes, edges, total, conv_total, pieces, out_sems,
):
    group, span, model = tokens.shape
    hidden = conv_input.shape[2]
    reach = left.shape[1]
    count = left.shape[0]
    size = group * span
    hb = order.hb
    fold = model // hidden
    step = pl.program_id(0)

    def vec(name, width):
        return table[ROW[name] : ROW[name] + 1, 0:width]

    def add(name, values, factor=1.0):
        width = values.shape[1]
        sums[ROW[name] : ROW[name] + 1, 0:width] += row_sum(values) * factor

    @pl.when(step == 0)
    def _():
        sums[...] = jnp.zeros_like(sums)
        total[...] = jnp.zeros_like(total)
        conv_total[...] = jnp.zeros_like(conv_total)
        before, behind = edge_windows(left[...], right[...], taps)
        for at, windows, first in ((0, before, 0), (reach, behind, taps // 2 + 1)):
            term = None
            for k, window in enumerate(windows):
                product = dot_nt(window, conv_t[first + k])
                term = product if term is None else term + product
            edges[:, at : at + reach] = term.reshape(count, reach, hidden)

    for g in range(group):
        at = step * group + g
        fill_padded(padded.at[g], left[at], conv_input[g], right[at])
    values = add_edges(part[...], edges[pl.ds(step * group, group)]) + vec("conv_bias", hidden)
    unit, inverse = normed(values)
    gain = vec("final_gain", hidden)
    three, slope = gelu_both(scaled(unit, gain, vec("final_shift", hidden)))
    threes[...] = three.astype(BF)
    incoming = cotangent[...].reshape(size, model)
    result = tokens[...].reshape(size, model).astype(F32) + dot_nt(threes[...], up_t[...])
    output[...] = (result + vec("up_bias", model)).astype(BF).reshape(group, span, model)
    twice = error[...].reshape(size, hidden) * slope
    grad, product = back_rows(twice, gain, unit, inverse)
    grad = grad.astype(BF)
    conv_out_grad[...] = grad.reshape(group, span, hidden)
    add("final_gain", product, 0.5)
    add("final_shift", twice, 0.5)
    add("conv_bias", grad.astype(F32))
    add("up_bias", incoming.astype(F32))
    total[...] += dot_tn(incoming, threes[...])
    windows = join(tap_windows(padded, range(taps), span))
    conv_total[...] += dot_nn(conv_out_grad[...].reshape(size, hidden).T, windows)

    @pl.when(step == pl.num_programs(0) - 1)
    def _():
        for b in range(grid.batch):
            for offset, spot, length in order.runs(b * hb, hb):
                rows = [
                    conv_total[spot : spot + length, k * hidden : (k + 1) * hidden].astype(BF)
                    for k in range(taps)
                ]
                for f in range(fold):
                    at = (b * fold + f) * hb + offset
                    rows.append(total[at : at + length].astype(BF))
                for s, piece in enumerate(wire_from_rows(order, rows)):
                    pieces[distance(grid, place, s, b) + (pl.ds(offset, length),)] = piece
        hand_out(pieces, (part_a, part_b, part_c, part_d), out_sems)


def stage_two(
    grid, order, taps, place, tokens, cotangent, conv_input, left, right, part, error, table,
    conv_t, up_t,
):
    count, span, model = tokens.shape
    hidden = conv_input.shape[2]
    reach = left.shape[1]
    group = group_of(count)
    fold = model // hidden
    pieces = piece_shape(grid, order.hb, (taps + fold) * order.hl)
    return pl.pallas_call(
        functools.partial(stage_two_kernel, grid, order, taps),
        out_shape=(
            sds((count, span, model), BF),
            sds((count, span, hidden), BF),
            sds((TABLE_ROWS, model), F32),
            *[sds(pieces, BF)] * 4,
        ),
        grid_spec=pltpu.PrefetchScalarGridSpec(
            num_scalar_prefetch=1,
            grid=(count // group,),
            in_specs=[
                rows_of((group, span, model)),
                rows_of((group, span, model)),
                rows_of((group, span, hidden)),
                whole((count, reach, hidden)),
                whole((count, reach, hidden)),
                rows_of((group, span, hidden)),
                rows_of((group, span, hidden)),
                whole(table.shape),
                whole(conv_t.shape),
                whole(up_t.shape),
            ],
            out_specs=[
                rows_of((group, span, model)),
                rows_of((group, span, hidden)),
                whole((TABLE_ROWS, model)),
                *[pl.BlockSpec(memory_space=pl.ANY)] * 4,
            ],
            scratch_shapes=[
                pltpu.VMEM((group, span + 2 * reach, hidden), BF),
                pltpu.VMEM((group * span, hidden), BF),
                pltpu.VMEM((count, 2 * reach, hidden), F32),
                pltpu.VMEM((model, hidden), F32),
                pltpu.VMEM((hidden, taps * hidden), F32),
                pltpu.VMEM((2, 2) + pieces, BF),
                pltpu.SemaphoreType.DMA((4,)),
            ],
        ),
        compiler_params=params(LIM2),
        cost_estimate=cost(
            2 * count * span * hidden * (taps * hidden + 2 * model),
            count * span * (6 * model + 12 * hidden),
        ),
        name="stage_two",
    )(
        place, tokens, cotangent, conv_input, left, right, part, error, table, conv_t, up_t,
    )


def inner_back_kernel(conv_out_grad, conv_t, part, padded):
    group, span, hidden = conv_out_grad.shape
    taps = conv_t.shape[0]
    reach = (padded.shape[1] - span) // 2

    @pl.when(pl.program_id(0) == 0)
    def _():
        padded[:, 0:reach] = jnp.zeros((group, reach, hidden), BF)
        padded[:, reach + span : 2 * reach + span] = jnp.zeros((group, reach, hidden), BF)

    padded[:, reach : reach + span] = conv_out_grad[...]
    windows = join(tap_windows(padded, reversed(range(taps)), span))
    part[...] = dot_nn(windows, conv_t[...].reshape(taps * hidden, hidden)).reshape(
        group, span, hidden
    )


def inner_back(conv_out_grad, conv_t, reach):
    count, span, hidden = conv_out_grad.shape
    taps = conv_t.shape[0]
    group = group_of(count)
    return pl.pallas_call(
        inner_back_kernel,
        out_shape=sds((count, span, hidden), F32),
        grid=(count // group,),
        in_specs=[rows_of((group, span, hidden)), whole(conv_t.shape)],
        out_specs=rows_of((group, span, hidden)),
        scratch_shapes=[pltpu.VMEM((group, span + 2 * reach, hidden), BF)],
        compiler_params=params(LIM3P),
        cost_estimate=cost(2 * count * span * hidden * taps * hidden, count * span * 6 * hidden),
        name="inner_back",
    )(conv_out_grad, conv_t)


def stage_three_kernel(
    start_ref, length_ref, part, narrow, left, right, table, sums_in, conv_t,
    narrow_grad, sums, edges,
):
    group, span, hidden = narrow.shape
    count, reach = left.shape[0], left.shape[1]
    taps = conv_t.shape[0]
    step = pl.program_id(0)

    def vec(name, width):
        return table[ROW[name] : ROW[name] + 1, 0:width]

    def add(name, values, factor=1.0):
        width = values.shape[1]
        sums[ROW[name] : ROW[name] + 1, 0:width] += row_sum(values) * factor

    @pl.when(step == 0)
    def _():
        sums[...] = sums_in[...]
        before, behind = edge_windows(left[...], right[...], taps)
        for at, windows, first in ((0, before, 0), (reach, behind, taps // 2 + 1)):
            term = None
            for k, window in enumerate(windows):
                product = dot_nn(window, conv_t[taps - 1 - first - k])
                term = product if term is None else term + product
            edges[:, at : at + reach] = term.reshape(count, reach, hidden)

    back = add_edges(part[...], edges[pl.ds(step * group, group)])
    back = back * valid_rows(start_ref, length_ref, group, span)
    unit, inverse = normed(narrow[...].reshape(group * span, hidden))
    gain = vec("middle_gain", hidden)
    _, slope = gelu_both(scaled(unit, gain, vec("middle_shift", hidden)))
    twice = back * slope
    low, product = back_rows(twice, gain, unit, inverse)
    low = low.astype(BF)
    narrow_grad[...] = low.reshape(group, span, hidden)
    add("middle_gain", product, 0.5)
    add("middle_shift", twice, 0.5)
    add("down_bias", low.astype(F32))


def stage_three(start, lengths, part, narrow, left, right, table, sums, conv_t):
    count, span, hidden = narrow.shape
    reach = left.shape[1]
    group = group_of(count)
    return pl.pallas_call(
        stage_three_kernel,
        out_shape=(sds((count, span, hidden), BF), sds(sums.shape, F32)),
        grid_spec=pltpu.PrefetchScalarGridSpec(
            num_scalar_prefetch=2,
            grid=(count // group,),
            in_specs=[
                rows_of((group, span, hidden)),
                rows_of((group, span, hidden)),
                whole((count, reach, hidden)),
                whole((count, reach, hidden)),
                whole(table.shape),
                whole(table.shape),
                whole(conv_t.shape),
            ],
            out_specs=[rows_of((group, span, hidden)), whole(sums.shape)],
            scratch_shapes=[pltpu.VMEM((count, 2 * reach, hidden), F32)],
        ),
        compiler_params=params(LIM3),
        cost_estimate=cost(2 * count * span * hidden * hidden, count * span * 10 * hidden),
        name="stage_three",
    )(start, lengths, part, narrow, left, right, table, sums, conv_t)


def stage_four_kernel(
    grid, order, begin, last, place, tokens, cotangent, narrow_grad, table, sums_in, down_t, *refs
):
    if last:
        hidden_one, narrow_all, refs = refs[0], refs[1], refs[2:]
    if not begin:
        refs = refs[1:]
    tokens_grad, sums, refs = refs[0], refs[1], refs[2:]
    span, model = tokens.shape[1], tokens.shape[2]
    hidden = narrow_grad.shape[2]
    hb, dl = order.hb, model // grid.seq
    step = pl.program_id(0)

    def vec(name, width):
        return table[ROW[name] : ROW[name] + 1, 0:width]

    def add(name, values, factor=1.0):
        width = values.shape[1]
        sums[ROW[name] : ROW[name] + 1, 0:width] += row_sum(values) * factor

    @pl.when(step == 0)
    def _():
        sums[...] = sums_in[...]
        if last:
            refs[4][...] = jnp.zeros_like(refs[4])

    if last:
        *parts, total, pieces, out_sems = refs
        size = narrow_all.shape[0] * span
        total[...] += dot_tn(
            narrow_all[...].reshape(size, hidden), hidden_one[...].reshape(size, model)
        )
    deep = dot_nn(narrow_grad[0], down_t[...])
    unit, inverse = normed(tokens[0].astype(F32))
    gain = vec("first_gain", model)
    _, slope = gelu_both(scaled(unit, gain, vec("first_shift", model)))
    twice = deep * slope
    grad, product = back_rows(twice, gain, unit, inverse)
    add("first_gain", product, 0.5)
    add("first_shift", twice, 0.5)
    tokens_grad[0] = (grad + cotangent[0].astype(F32)).astype(BF)

    if last:

        @pl.when(step == pl.num_programs(0) - 1)
        def _():
            wide = model // grid.batch
            sub = lax.broadcasted_iota(jnp.int32, (TABLE_ROWS, dl), 0)
            for b in range(grid.batch):
                upper = sums[:, b * wide : (b + 1) * wide]
                runs = order.runs(b * hb, hb)
                lower = join([sums[:, spot : spot + length] for _, spot, length in runs])
                if wide < dl:
                    upper = join([upper, jnp.zeros((TABLE_ROWS, dl - wide), F32)])
                lower = join([lower, jnp.zeros((TABLE_ROWS, dl - hb), F32)])
                tail = jnp.where(sub < WIDE_ROWS, upper, lower).astype(BF)
                for s in range(grid.seq):
                    to = distance(grid, place, s, b)
                    for offset, spot, length in runs:
                        pieces[to + (pl.ds(offset, length),)] = total[
                            spot : spot + length, s * dl : (s + 1) * dl
                        ].astype(BF)
                    pieces[to + (pl.ds(hb, 16),)] = tail
            hand_out(pieces, parts, out_sems)


def stage_four(
    grid, order, first, part, begin, last, place, tokens, cotangent, hidden_one, narrow_grad,
    table, sums, down_t, grad_in,
):
    count, span, model = tokens.shape
    hidden = narrow_grad.shape[2]
    pieces = piece_shape(grid, order.hb + 16, model // grid.seq)

    def part_of(block):
        return pl.BlockSpec(block, lambda i, *_: (first + i,) + (0,) * (len(block) - 1))

    in_specs = [
        part_of((1, span, model)),
        part_of((1, span, model)),
        part_of((1, span, hidden)),
        whole(table.shape),
        whole(table.shape),
        whole(down_t.shape),
    ]
    inputs = [tokens, cotangent, narrow_grad, table, sums, down_t]
    out_shape = [sds((count, span, model), BF), sds(table.shape, F32)]
    out_specs = [part_of((1, span, model)), whole(table.shape)]
    scratch = []
    if last:
        share = count // part
        in_specs += [rows_of((share, span, model)), rows_of((share, span, hidden))]
        inputs += [hidden_one, narrow_grad]
        out_shape += [sds(pieces, BF)] * 4
        out_specs += [pl.BlockSpec(memory_space=pl.ANY)] * 4
        scratch = [
            pltpu.VMEM((hidden, model), F32),
            pltpu.VMEM((2, 2) + pieces, BF),
            pltpu.SemaphoreType.DMA((4,)),
        ]
    aliases = {}
    if not begin:
        in_specs.append(pl.BlockSpec(memory_space=pl.ANY))
        inputs.append(grad_in)
        aliases = {len(inputs): 0}
    return pl.pallas_call(
        functools.partial(stage_four_kernel, grid, order, begin, last),
        out_shape=tuple(out_shape),
        grid_spec=pltpu.PrefetchScalarGridSpec(
            num_scalar_prefetch=1,
            grid=(part,),
            in_specs=in_specs,
            out_specs=out_specs,
            scratch_shapes=scratch,
        ),
        input_output_aliases=aliases,
        compiler_params=params(LIM4),
        cost_estimate=cost(
            4 * part * span * hidden * model, part * span * (8 * model + 2 * hidden)
        ),
        name="stage_four",
    )(place, *inputs)


def halos(cells, reach):
    count = lax.axis_size("seq")
    left = lax.ppermute(
        cells[:, cells.shape[1] - reach :], "seq", [(i, i + 1) for i in range(count - 1)]
    )
    right = lax.ppermute(cells[:, :reach], "seq", [(i + 1, i) for i in range(count - 1)])
    return left, right


def after(value, *others):
    return lax.optimization_barrier((value,) + others)[0]


def body(
    grid,
    tokens,
    lengths,
    first_gain,
    first_shift,
    down_weight,
    down_bias,
    middle_gain,
    middle_shift,
    conv_weight,
    conv_bias,
    final_gain,
    final_shift,
    up_weight,
    up_bias,
    cotangent,
):
    shape = tokens.shape
    span, model = shape[2], shape[3]
    count = shape[0] * shape[1]
    taps = conv_weight.shape[0]
    hidden = down_weight.shape[1] * grid.batch
    order = Order(grid, hidden)
    hb, hl, dl = order.hb, order.hl, down_weight.shape[0]
    fold = model // hidden
    reach = (taps - 1) // 2 * DILATION

    tokens = tokens.reshape(count, span, model)
    cotangent = cotangent.reshape(count, span, model)
    lengths = lengths.reshape(count)
    place = jnp.stack(grid.here()).astype(jnp.int32)
    start = (lax.axis_index("seq") * span).astype(jnp.int32).reshape(1)

    vectors = {
        "first_gain": first_gain,
        "first_shift": first_shift,
        "up_bias": up_bias,
        "down_bias": down_bias,
        "middle_gain": middle_gain,
        "middle_shift": middle_shift,
        "conv_bias": conv_bias,
        "final_gain": final_gain,
        "final_shift": final_shift,
    }
    first_piece = pack_first(order, down_weight.T, [vectors[name] for name in WIDE + NARROW])
    second_piece = pack_second(order, after(conv_weight, first_piece), up_weight)

    def meet(*groups):
        flat = lax.optimization_barrier(tuple(value for group in groups for value in group))
        found, at = [], 0
        for group in groups:
            found.append(flat[at : at + len(group)])
            at += len(group)
        return found

    first = grid.gather_deep(first_piece)
    neighbour, second_piece = lax.optimization_barrier((first[1], second_piece))
    first[1] = neighbour
    second = grid.halves(grid.gather_deep(second_piece))
    one, two = grid.gather_near(*grid.halves(first))
    far_one, far_two = grid.gather_far(one, two)
    first = [one, *far_one, two, *far_two]
    first, second = meet(first, second)
    first = [*first, *grid.gather_core(first)]
    near = grid.gather_near(*second)
    near, first = meet(near, first)
    near_other = grid.gather_core(near)
    far_one, far_two = grid.gather_far(*near)
    hidden_one, narrow, conv_input, down_t, table = stage_one(
        grid, order, place, start, lengths, tokens, first
    )
    far_one, far_two, near_other, (conv_input,) = meet(
        far_one, far_two, near_other, (conv_input,)
    )
    left, right = halos(conv_input, reach)
    far_one_other, far_two_other = grid.gather_core(far_one), grid.gather_core(far_two)
    second = [near[0], *far_one, near[1], *far_two]
    second += [near_other[0], *far_one_other, near_other[1], *far_two_other]
    part, error, conv_t, up_t = inner(
        grid, order, taps, reach, place, cotangent, conv_input, second
    )
    block_output, conv_out_grad, sums, *rest = stage_two(
        grid, order, taps, place, tokens, cotangent, conv_input, left, right, part, error, table,
        conv_t, up_t,
    )

    left, right = halos(conv_out_grad, reach)
    rest = grid.reduce_core(*rest)
    part = inner_back(conv_out_grad, conv_t, reach)
    rest, (sums, left, right, part) = meet(rest, (sums, left, right, part))

    rest = grid.reduce_far(*rest)
    narrow_grad, sums = stage_three(
        start, lengths, part, narrow, left, right, table, sums, conv_t
    )
    half = count // 2
    tokens_grad, sums = stage_four(
        grid, order, 0, half, True, False, place, tokens, cotangent, hidden_one, narrow_grad,
        table, sums, down_t, None,
    )
    rest, (sums,) = meet(rest, (sums,))

    rest = grid.reduce_near(*rest)
    tokens_grad, sums, *down = stage_four(
        grid, order, half, half, False, True, place, tokens, cotangent, hidden_one, narrow_grad,
        table, sums, down_t, tokens_grad,
    )
    rest, down = meet(rest, down)

    down = grid.reduce_core(*down)
    down, rest = meet(down, rest)
    down = grid.reduce_far(*down)
    rest = grid.reduce_deep(*rest)
    down = grid.reduce_near(*down)
    down = grid.reduce_deep(*down)
    conv_grad, up_grad = unpack_rest(order, taps, fold, rest)
    down_grad, tail = unpack_first(order, down)
    grads = {name: tail[ROW[name], : vectors[name].shape[0]] for name in vectors}
    return (
        block_output.reshape(shape),
        tokens_grad.reshape(shape),
        grads["first_gain"],
        grads["first_shift"],
        down_grad.T,
        grads["down_bias"],
        grads["middle_gain"],
        grads["middle_shift"],
        conv_grad,
        grads["conv_bias"],
        grads["final_gain"],
        grads["final_shift"],
        up_grad,
        grads["up_bias"],
    )


def solution(mesh):
    grid = Grid(mesh.shape["seq"], mesh.shape["batch"])
    return jax.shard_map(
        functools.partial(body, grid),
        mesh=mesh,
        in_specs=(
            P(None, "batch", "seq", None),
            P(None, "batch"),
            P("batch"),
            P("batch"),
            P("seq", "batch"),
            P("batch"),
            P("batch"),
            P("batch"),
            P(None, "seq", "batch"),
            P("batch"),
            P("batch"),
            P("batch"),
            P("seq", "batch"),
            P("batch"),
            P(None, "batch", "seq", None),
        ),
        out_specs=(
            P(None, "batch", "seq", None),
            P(None, "batch", "seq", None),
            P("batch"),
            P("batch"),
            P("seq", "batch"),
            P("batch"),
            P("batch"),
            P("batch"),
            P(None, "seq", "batch"),
            P("batch"),
            P("batch"),
            P("batch"),
            P("seq", "batch"),
            P("batch"),
        ),
        check_vma=False,
    )
```

profile of v0, /device:TPU:0, one launch (start us, length us, event | category | flops | bytes accessed | tf_op | source)
XLA Modules:
  0.0 227.8 jit_solution(11431612295620282671)
XLA Ops:
  2.2 3.0 %collective-permute-start = (bf16[96,320]{1,0:T(8,128)(2,1)}, bf16[96,320]{1,0:T(8,128)(2,1)S(1)}, u32[]{:S(2)}, u32[]{:S(2)}) collective-permute-start(bf16[96,320]{1,0:T(8,128)(2,1)} %pack_first.1), channel_id=1, source_target_pairs={{0,2},{1,3},{2,4},{3,5},{4,6},{5,7},{6,0},{7,1},{8,10},{9,11},{10,... | collective-permute-start | bytes 184328 | tf_op jit(solution)/shard_map/ppermute | solution.py:58
  5.2 2.0 collective-permute-start.4
  8.3 2.0 pack_second.1
  11.2 1.8 collective-permute-start.1
  16.1 2.0 collective-permute-start.9
  21.5 2.0 collective-permute-done.9
  23.5 9.6 %collective-permute-done.8 = bf16[80,1120]{1,0:T(8,128)(2,1)S(1)} collective-permute-done((bf16[80,1120]{1,0:T(8,128)(2,1)}, bf16[80,1120]{1,0:T(8,128)(2,1)S(1)}, u32[]{:S(2)}, u32[]{:S(2)}) %collective-permute-start.8) | collective-permute-done | bytes 179232 | tf_op jit(solution)/shard_map/ppermute | solution.py:58
  35.9 7.0 %collective-permute-done.10 = bf16[2,80,1120]{2,1,0:T(8,128)(2,1)S(1)} collective-permute-done((bf16[2,80,1120]{2,1,0:T(8,128)(2,1)S(1)}, bf16[2,80,1120]{2,1,0:T(8,128)(2,1)S(1)}, u32[]{:S(2)}, u32[]{:S(2)}) %collective-permute-start.10) | collective-permute-done | bytes 358432 | tf_op jit(solution)/shard_map/ppermute | solution.py:58
  48.7 15.9 %stage_one.1 = (bf16[8,256,1280]{2,1,0:T(8,128)(2,1)}, f32[8,256,640]{2,1,0:T(8,128)}, bf16[8,256,640]{2,1,0:T(8,128)(2,1)}, bf16[640,1280]{1,0:T(8,128)(2,1)}, f32[16,1280]{1,0:T(8,128)}) custom-call(s32[4]{0:T(128)} %pad_add_fusion.place, s32[1]{0:T(128)} %bitcast.23.start_ref, s32[8]{0:T(128)} %reshape.65.length_ref, bf16[8,256,1280]{2,1,0:T(8,128)(2,1)} %bitcast.104, ...), custom_call_target="tpu_custom_call" | custom-call | flops 3355443200 | bytes 18350080 | tf_op jit(solution)/shard_map/stage_one/pallas_call | solution.py:453
  68.4 4.6 %collective-permute-start.20 = (bf16[8,32,640]{2,1,0:T(8,128)(2,1)S(1)}, bf16[8,32,640]{2,1,0:T(8,128)(2,1)S(1)}, u32[]{:S(2)}, u32[]{:S(2)}) collective-permute-start(bf16[8,32,640]{2,1,0:T(8,128)(2,1)S(1)} %get-tuple-element.161), channel_id=1, source_target_pairs={{0,8},{8,16},{16,24},{1,9},{9,17},{17,25},{2,10},{10,18},{18,26},{... | collective-permute-start | bytes 983048 | tf_op jit(solution)/shard_map/ppermute | solution.py:985
  73.9 23.4 %inner.1 = (f32[8,256,640]{2,1,0:T(8,128)}, f32[8,256,640]{2,1,0:T(8,128)}, bf16[5,640,640]{2,1,0:T(8,128)(2,1)}, bf16[1280,640]{1,0:T(8,128)(2,1)}) custom-call(s32[4]{0:T(128)} %pad_add_fusion.place, bf16[8,256,1280]{2,1,0:T(8,128)(2,1)} %bitcast.108, bf16[8,256,640]{2,1,0:T(8,128)(2,1)} %get-tuple-element.106.conv_input, ...), custom_call_target="tpu_custom_call" | custom-call | flops 11744051200 | bytes 18350080 | tf_op jit(solution)/shard_map/inner/pallas_call | solution.py:585
  98.2 36.3 %stage_two.1 = (bf16[8,256,1280]{2,1,0:T(8,128)(2,1)}, bf16[8,256,640]{2,1,0:T(8,128)(2,1)}, f32[16,1280]{1,0:T(8,128)}, bf16[2,2,2,80,1120]{4,3,2,1,0:T(8,128)(...) custom-call(s32[4]{0:T(128)} %pad_add_fusion.place, ...), custom_call_target="tpu_custom_call" | custom-call | flops 15099494400 | bytes 31457280 | tf_op jit(solution)/shard_map/stage_two/pallas_call | solution.py:706
  137.0 4.6 %collective-permute-start.26 = (bf16[8,32,640]{2,1,0:T(8,128)(2,1)S(1)}, bf16[8,32,640]{2,1,0:T(8,128)(2,1)S(1)}, u32[]{:S(2)}, u32[]{:S(2)}) collective-permute-start(bf16[8,32,640]{2,1,0:T(8,128)(2,1)S(1)} %get-tuple-element.159), channel_id=1, source_target_pairs={{0,8},{8,16},{16,24},{1,9},{9,17},{17,25},{2,10},{10,18},{18,26},{... | collective-permute-start | bytes 983048 | tf_op jit(solution)/shard_map/ppermute | solution.py:985
  141.7 14.8 %inner_back.1.part = f32[8,256,640]{2,1,0:T(8,128)} custom-call(bf16[8,256,640]{2,1,0:T(8,128)(2,1)} %get-tuple-element.122.conv_out_grad, bf16[5,640,640]{2,1,0:T(8,128)(2,1)} %get-tuple-element.114.conv_t), custom_call_target="tpu_custom_call" | custom-call | flops 8388608000 | bytes 7864320 | tf_op jit(solution)/shard_map/inner_back/pallas_call | solution.py:777
  157.4 2.6 %collective-permute-start.29 = (bf16[2,2,80,1120]{3,2,1,0:T(8,128)(2,1)S(1)}, bf16[2,2,80,1120]{3,2,1,0:T(8,128)(2,1)S(1)}, u32[]{:S(2)}, u32[]{:S(2)}) collective-permute-start(bf16[2,2,80,1120]{3,2,1,0:T(8,128)(2,1)S(1)} %slice_bitcast_fusion), channel_id=1, source_target_pairs={{0,8},{1,9},{2,10},{3,11},{4,12},{5,13},{6,14},{7,15},{8,0},{9,1},... | collective-permute-start | bytes 2150408 | tf_op jit(solution)/shard_map/ppermute | solution.py:58
  160.3 9.6 %stage_three.1 = (bf16[8,256,640]{2,1,0:T(8,128)(2,1)S(1)}, f32[16,1280]{1,0:T(8,128)S(1)}) custom-call(s32[1]{0:T(128)} %bitcast.23.start_ref, s32[8]{0:T(128)S(1)} %copy-done.7, f32[8,256,640]{2,1,0:T(8,128)S(1)} %copy-done.2, f32[8,256,640]{2,1,0:T(8,128)} %get-tuple-element.124.narrow, bf16[8,32,640]{2,1,0:T(8,128)(2,1)S(1)} %collective-permute-done.26.left, ...), custom_call_target="tpu_custom_call" | custom-call | flops 1677721600 | bytes 13107200 | tf_op jit(solution)/shard_map/stage_three/pallas_call | solution.py:835
  169.9 9.5 %stage_four.2 = (bf16[8,256,1280]{2,1,0:T(8,128)(2,1)}, f32[16,1280]{1,0:T(8,128)S(1)}) custom-call(s32[4]{0:T(128)S(1)} %copy-done.6, bf16[8,256,1280]{2,1,0:T(8,128)(2,1)} %bitcast.106, bf16[8,256,1280]{2,1,0:T(8,128)(2,1)} %bitcast.110, bf16[8,256,640]{2,1,0:T(8,128)(2,1)S(1)} %get-tuple-element.128.narrow_grad.refs_1_, f32[16,1280]{1,0:T(8,128)S(1)} %copy-done.4, ...), custom_call_target="tpu_custom_call" | custom-call | flops 3355443200 | bytes 11796480 | tf_op jit(solution)/shard_map/stage_four/pallas_call | solution.py:964
  179.9 2.0 collective-permute-start.31
  182.6 14.3 %stage_four.3 = (bf16[8,256,1280]{2,1,0:T(8,128)(2,1)}, f32[16,1280]{1,0:T(8,128)}, bf16[2,2,2,96,320]{4,3,2,1,0:T(8,128)(2,1)S(1)}, bf16[2,2,2,96,320]{4,3,2,1,...) custom-call(s32[4]{0:T(128)S(1)} %copy-done.6, ...), custom_call_target="tpu_custom_call", output_to_operand_aliasing={{0}: (9, {})} | custom-call | flops 3355443200 | bytes 11796480 | tf_op jit(solution)/shard_map/stage_four/pallas_call | solution.py:964
  204.7 3.3 %collective-permute-start.42 = (bf16[80,1120]{1,0:T(8,128)(2,1)S(1)}, bf16[80,1120]{1,0:T(8,128)(2,1)S(1)}, u32[]{:S(2)}, u32[]{:S(2)}) collective-permute-start(bf16[80,1120]{1,0:T(8,128)(2,1)S(1)} %get-tuple-element.163), channel_id=1, source_target_pairs={{0,4},{1,5},{2,6},{3,7},{4,0},{5,1},{6,2},{7,3},{8,12},{9,13},{10,... | collective-permute-start | bytes 537608 | tf_op jit(solution)/shard_map/ppermute | solution.py:58
  209.7 2.1 collective-permute-start.38
  212.2 2.7 %collective-permute-done.38 = bf16[2,96,320]{2,1,0:T(8,128)(2,1)S(1)} collective-permute-done((bf16[2,96,320]{2,1,0:T(8,128)(2,1)S(1)}, bf16[2,96,320]{2,1,0:T(8,128)(2,1)S(1)}, u32[]{:S(2)}, u32[]{:S(2)}) %collective-permute-start.38) | collective-permute-done | bytes 122912 | tf_op jit(solution)/shard_map/ppermute | solution.py:58
  217.1 3.3 %collective-permute-start.39 = (bf16[96,320]{1,0:T(8,128)(2,1)S(1)}, bf16[96,320]{1,0:T(8,128)(2,1)S(1)}, u32[]{:S(2)}, u32[]{:S(2)}) collective-permute-start(bf16[96,320]{1,0:T(8,128)(2,1)S(1)} %get-tuple-element.167), channel_id=1, source_target_pairs={{0,4},{1,5},{2,6},{3,7},{4,0},{5,1},{6,2},{7,3},{8,12},{9,13},{10,... | collective-permute-start | bytes 184328 | tf_op jit(solution)/shard_map/ppermute | solution.py:58
  221.6 2.7 %collective-permute-done.42.refs_2_ = bf16[80,1120]{1,0:T(8,128)(2,1)S(1)} collective-permute-done((bf16[80,1120]{1,0:T(8,128)(2,1)S(1)}, bf16[80,1120]{1,0:T(8,128)(2,1)S(1)}, u32[]{:S(2)}, u32[]{:S(2)}) %collective-permute-start.42) | collective-permute-done | bytes 179232 | tf_op jit(solution)/shard_map/ppermute | solution.py:58
  (167 shorter events, 45.5 us)
Async XLA Ops:
  18.1 15.1 %collective-permute-start.8 = (bf16[80,1120]{1,0:T(8,128)(2,1)}, bf16[80,1120]{1,0:T(8,128)(2,1)S(1)}, u32[]{:S(2)}, u32[]{:S(2)}) collective-permute-start(bf16[80,1120]{1,0:T(8,128)(2,1)} %pack_second.1), channel_id=1, source_target_pairs={{0,4},{1,5},{2,6},{3,7},{4,0},{5,1},{6,2},{7,3},{8,12},{9,13},{10,... | collective-permute-start | bytes 537608 | tf_op jit(solution)/shard_map/ppermute | solution.py:58
  18.1 15.1 %collective-permute-start.7 = (bf16[80,1120]{1,0:T(8,128)(2,1)}, bf16[80,1120]{1,0:T(8,128)(2,1)S(1)}, u32[]{:S(2)}, u32[]{:S(2)}) collective-permute-start(bf16[80,1120]{1,0:T(8,128)(2,1)} %pack_second.1), channel_id=1, source_target_pairs={{0,2},{1,3},{2,4},{3,5},{4,6},{5,7},{6,0},{7,1},{8,10},{9,11},{10,... | collective-permute-start | bytes 537608 | tf_op jit(solution)/shard_map/ppermute | solution.py:58
  18.7 14.6 %collective-permute-start.2 = (bf16[2,2,96,320]{3,2,1,0:T(8,128)(2,1)S(1)}, bf16[2,2,96,320]{3,2,1,0:T(8,128)(2,1)S(1)}, u32[]{:S(2)}, u32[]{:S(2)}) collective-permute-start(bf16[2,2,96,320]{3,2,1,0:T(8,128)(2,1)S(1)} %pad_maximum_fusion.4.refs_0_), channel_id=1, source_target_pairs={{0,16},{1,17},{2,18},{3,19},{4,20},{5,21},{6,22},{7,23},{8,24},{9,... | collective-permute-start | bytes 737288 | tf_op jit(solution)/shard_map/ppermute | solution.py:58
  20.2 13.1 %collective-permute-start.6 = (bf16[2,2,96,320]{3,2,1,0:T(8,128)(2,1)S(1)}, bf16[2,2,96,320]{3,2,1,0:T(8,128)(2,1)S(1)}, u32[]{:S(2)}, u32[]{:S(2)}) collective-permute-start(bf16[2,2,96,320]{3,2,1,0:T(8,128)(2,1)S(1)} %pad_maximum_fusion.5.refs_2_), channel_id=1, source_target_pairs={{0,8},{1,9},{2,10},{3,11},{4,12},{5,13},{6,14},{7,15},{8,0},{9,1},... | collective-permute-start | bytes 737288 | tf_op jit(solution)/shard_map/ppermute | solution.py:58
  33.3 9.6 %collective-permute-start.10 = (bf16[2,80,1120]{2,1,0:T(8,128)(2,1)S(1)}, bf16[2,80,1120]{2,1,0:T(8,128)(2,1)S(1)}, u32[]{:S(2)}, u32[]{:S(2)}) collective-permute-start(bf16[2,80,1120]{2,1,0:T(8,128)(2,1)S(1)} %pad_maximum_fusion.2), channel_id=1, source_target_pairs={{0,8},{1,9},{2,10},{3,11},{4,12},{5,13},{6,14},{7,15},{8,0},{9,1},... | collective-permute-start | bytes 1075208 | tf_op jit(solution)/shard_map/ppermute | solution.py:58
  45.7 18.8 %collective-permute-start.18 = (bf16[2,2,80,1120]{3,2,1,0:T(8,128)(2,1)S(1)}, bf16[2,2,80,1120]{3,2,1,0:T(8,128)(2,1)S(1)}, u32[]{:S(2)}, u32[]{:S(2)}) collective-permute-start(bf16[2,2,80,1120]{3,2,1,0:T(8,128)(2,1)S(1)} %pad_maximum_fusion.refs_0_), channel_id=1, source_target_pairs={{0,1},{1,0},{2,3},{3,2},{4,5},{5,4},{6,7},{7,6},{8,9},{9,8},{10,11... | collective-permute-start | bytes 2150408 | tf_op jit(solution)/shard_map/ppermute | solution.py:58
  45.7 18.9 %collective-permute-start.16 = (bf16[2,2,80,1120]{3,2,1,0:T(8,128)(2,1)S(1)}, bf16[2,2,80,1120]{3,2,1,0:T(8,128)(2,1)S(1)}, u32[]{:S(2)}, u32[]{:S(2)}) collective-permute-start(bf16[2,2,80,1120]{3,2,1,0:T(8,128)(2,1)S(1)} %pad_maximum_fusion.refs_0_), channel_id=1, source_target_pairs={{0,16},{1,17},{2,18},{3,19},{4,20},{5,21},{6,22},{7,23},{8,24},{9,... | collective-permute-start | bytes 2150408 | tf_op jit(solution)/shard_map/ppermute | solution.py:58
  46.5 18.2 %collective-permute-start.19 = (bf16[2,2,80,1120]{3,2,1,0:T(8,128)(2,1)S(1)}, bf16[2,2,80,1120]{3,2,1,0:T(8,128)(2,1)}, u32[]{:S(2)}, u32[]{:S(2)}) collective-permute-start(bf16[2,2,80,1120]{3,2,1,0:T(8,128)(2,1)S(1)} %pad_maximum_fusion.1.refs_2_), channel_id=1, source_target_pairs={{0,1},{1,0},{2,3},{3,2},{4,5},{5,4},{6,7},{7,6},{8,9},{9,8},{10,11... | collective-permute-start | bytes 2150408 | tf_op jit(solution)/shard_map/ppermute | solution.py:58
  46.5 19.0 %collective-permute-start.17 = (bf16[2,2,80,1120]{3,2,1,0:T(8,128)(2,1)S(1)}, bf16[2,2,80,1120]{3,2,1,0:T(8,128)(2,1)}, u32[]{:S(2)}, u32[]{:S(2)}) collective-permute-start(bf16[2,2,80,1120]{3,2,1,0:T(8,128)(2,1)S(1)} %pad_maximum_fusion.1.refs_2_), channel_id=1, source_target_pairs={{0,8},{1,9},{2,10},{3,11},{4,12},{5,13},{6,14},{7,15},{8,0},{9,1},... | collective-permute-start | bytes 2150408 | tf_op jit(solution)/shard_map/ppermute | solution.py:58
  67.1 30.2 %collective-permute-start.21 = (bf16[8,32,640]{2,1,0:T(8,128)(2,1)S(1)}, bf16[8,32,640]{2,1,0:T(8,128)(2,1)S(1)}, u32[]{:S(2)}, u32[]{:S(2)}) collective-permute-start(bf16[8,32,640]{2,1,0:T(8,128)(2,1)S(1)} %get-tuple-element.160), channel_id=1, source_target_pairs={{8,0},{16,8},{24,16},{9,1},{17,9},{25,17},{10,2},{18,10},{26,18},{... | collective-permute-start | bytes 983048 | tf_op jit(solution)/shard_map/ppermute | solution.py:988
  68.4 28.9 %collective-permute-start.20 = (bf16[8,32,640]{2,1,0:T(8,128)(2,1)S(1)}, bf16[8,32,640]{2,1,0:T(8,128)(2,1)S(1)}, u32[]{:S(2)}, u32[]{:S(2)}) collective-permute-start(bf16[8,32,640]{2,1,0:T(8,128)(2,1)S(1)} %get-tuple-element.161), channel_id=1, source_target_pairs={{0,8},{8,16},{16,24},{1,9},{9,17},{17,25},{2,10},{10,18},{18,26},{... | collective-permute-start | bytes 983048 | tf_op jit(solution)/shard_map/ppermute | solution.py:985
  134.5 22.0 %collective-permute-start.24 = (bf16[2,2,2,80,1120]{4,3,2,1,0:T(8,128)(2,1)}, bf16[2,2,2,80,1120]{4,3,2,1,0:T(8,128)(2,1)S(1)}, u32[]{:S(2)}, u32[]{:S(2)}) collective-permute-start(bf16[2,2,2,80,1120]{4,3,2,1,0:T(8,128)(2,1)} %get-tuple-element.118), channel_id=1, source_target_pairs={{0,1},{1,0},{2,3},{3,2},{4,5},{5,4},{6,7},{7,6},{8,9},{9,8},{10,11... | collective-permute-start | bytes 4300808 | tf_op jit(solution)/shard_map/ppermute | solution.py:58
  135.7 21.5 %collective-permute-start.27 = (bf16[8,32,640]{2,1,0:T(8,128)(2,1)S(1)}, bf16[8,32,640]{2,1,0:T(8,128)(2,1)S(1)}, u32[]{:S(2)}, u32[]{:S(2)}) collective-permute-start(bf16[8,32,640]{2,1,0:T(8,128)(2,1)S(1)} %get-tuple-element.158), channel_id=1, source_target_pairs={{8,0},{16,8},{24,16},{9,1},{17,9},{25,17},{10,2},{18,10},{26,18},{... | collective-permute-start | bytes 983048 | tf_op jit(solution)/shard_map/ppermute | solution.py:988
  137.0 20.3 %collective-permute-start.26 = (bf16[8,32,640]{2,1,0:T(8,128)(2,1)S(1)}, bf16[8,32,640]{2,1,0:T(8,128)(2,1)S(1)}, u32[]{:S(2)}, u32[]{:S(2)}) collective-permute-start(bf16[8,32,640]{2,1,0:T(8,128)(2,1)S(1)} %get-tuple-element.159), channel_id=1, source_target_pairs={{0,8},{8,16},{16,24},{1,9},{9,17},{17,25},{2,10},{10,18},{18,26},{... | collective-permute-start | bytes 983048 | tf_op jit(solution)/shard_map/ppermute | solution.py:985
  141.6 15.3 %collective-permute-start.25 = (bf16[2,2,2,80,1120]{4,3,2,1,0:T(8,128)(2,1)}, bf16[2,2,2,80,1120]{4,3,2,1,0:T(8,128)(2,1)S(1)}, u32[]{:S(2)}, u32[]{:S(2)}) collective-permute-start(bf16[2,2,2,80,1120]{4,3,2,1,0:T(8,128)(2,1)} %get-tuple-element.120), channel_id=1, source_target_pairs={{0,1},{1,0},{2,3},{3,2},{4,5},{5,4},{6,7},{7,6},{8,9},{9,8},{10,11... | collective-permute-start | bytes 4300808 | tf_op jit(solution)/shard_map/ppermute | solution.py:58
  157.4 22.1 %collective-permute-start.29 = (bf16[2,2,80,1120]{3,2,1,0:T(8,128)(2,1)S(1)}, bf16[2,2,80,1120]{3,2,1,0:T(8,128)(2,1)S(1)}, u32[]{:S(2)}, u32[]{:S(2)}) collective-permute-start(bf16[2,2,80,1120]{3,2,1,0:T(8,128)(2,1)S(1)} %slice_bitcast_fusion), channel_id=1, source_target_pairs={{0,8},{1,9},{2,10},{3,11},{4,12},{5,13},{6,14},{7,15},{8,0},{9,1},... | collective-permute-start | bytes 2150408 | tf_op jit(solution)/shard_map/ppermute | solution.py:58
  160.1 19.6 %collective-permute-start.28 = (bf16[2,2,80,1120]{3,2,1,0:T(8,128)(2,1)S(1)}, bf16[2,2,80,1120]{3,2,1,0:T(8,128)(2,1)S(1)}, u32[]{:S(2)}, u32[]{:S(2)}) collective-permute-start(bf16[2,2,80,1120]{3,2,1,0:T(8,128)(2,1)S(1)} %slice_bitcast_fusion.1), channel_id=1, source_target_pairs={{0,16},{1,17},{2,18},{3,19},{4,20},{5,21},{6,22},{7,23},{8,24},{9,... | collective-permute-start | bytes 2150408 | tf_op jit(solution)/shard_map/ppermute | solution.py:58
  179.9 17.1 %collective-permute-start.31 = (bf16[2,80,1120]{2,1,0:T(8,128)(2,1)S(1)}, bf16[2,80,1120]{2,1,0:T(8,128)(2,1)S(1)}, u32[]{:S(2)}, u32[]{:S(2)}) collective-permute-start(bf16[2,80,1120]{2,1,0:T(8,128)(2,1)S(1)} %slice_bitcast_fusion.2), channel_id=1, source_target_pairs={{0,16},{1,17},{2,18},{3,19},{4,20},{5,21},{6,22},{7,23},{8,24},{9,... | collective-permute-start | bytes 1075208 | tf_op jit(solution)/shard_map/ppermute | solution.py:58
  181.9 15.2 %collective-permute-start.30 = (bf16[2,80,1120]{2,1,0:T(8,128)(2,1)S(1)}, bf16[2,80,1120]{2,1,0:T(8,128)(2,1)S(1)}, u32[]{:S(2)}, u32[]{:S(2)}) collective-permute-start(bf16[2,80,1120]{2,1,0:T(8,128)(2,1)S(1)} %slice_bitcast_fusion.3), channel_id=1, source_target_pairs={{0,8},{1,9},{2,10},{3,11},{4,12},{5,13},{6,14},{7,15},{8,0},{9,1},... | collective-permute-start | bytes 1075208 | tf_op jit(solution)/shard_map/ppermute | solution.py:58
  200.3 20.1 %collective-permute-start.41 = (bf16[80,1120]{1,0:T(8,128)(2,1)S(1)}, bf16[80,1120]{1,0:T(8,128)(2,1)S(1)}, u32[]{:S(2)}, u32[]{:S(2)}) collective-permute-start(bf16[80,1120]{1,0:T(8,128)(2,1)S(1)} %get-tuple-element.164), channel_id=1, source_target_pairs={{0,6},{1,7},{2,0},{3,1},{4,2},{5,3},{6,4},{7,5},{8,14},{9,15},{10,... | collective-permute-start | bytes 537608 | tf_op jit(solution)/shard_map/ppermute | solution.py:58
  202.1 9.6 %collective-permute-start.34 = (bf16[2,2,96,320]{3,2,1,0:T(8,128)(2,1)S(1)}, bf16[2,2,96,320]{3,2,1,0:T(8,128)(2,1)S(1)}, u32[]{:S(2)}, u32[]{:S(2)}) collective-permute-start(bf16[2,2,96,320]{3,2,1,0:T(8,128)(2,1)S(1)} %slice_bitcast_fusion.5), channel_id=1, source_target_pairs={{0,16},{1,17},{2,18},{3,19},{4,20},{5,21},{6,22},{7,23},{8,24},{9,... | collective-permute-start | bytes 737288 | tf_op jit(solution)/shard_map/ppermute | solution.py:58
  202.9 18.7 %collective-permute-start.43 = (bf16[80,1120]{1,0:T(8,128)(2,1)S(1)}, bf16[80,1120]{1,0:T(8,128)(2,1)S(1)}, u32[]{:S(2)}, u32[]{:S(2)}) collective-permute-start(bf16[80,1120]{1,0:T(8,128)(2,1)S(1)} %get-tuple-element.162), channel_id=1, source_target_pairs={{0,2},{1,3},{2,4},{3,5},{4,6},{5,7},{6,0},{7,1},{8,10},{9,11},{10,... | collective-permute-start | bytes 537608 | tf_op jit(solution)/shard_map/ppermute | solution.py:58
  204.7 19.7 %collective-permute-start.42 = (bf16[80,1120]{1,0:T(8,128)(2,1)S(1)}, bf16[80,1120]{1,0:T(8,128)(2,1)S(1)}, u32[]{:S(2)}, u32[]{:S(2)}) collective-permute-start(bf16[80,1120]{1,0:T(8,128)(2,1)S(1)} %get-tuple-element.163), channel_id=1, source_target_pairs={{0,4},{1,5},{2,6},{3,7},{4,0},{5,1},{6,2},{7,3},{8,12},{9,13},{10,... | collective-permute-start | bytes 537608 | tf_op jit(solution)/shard_map/ppermute | solution.py:58
  215.0 10.5 %collective-permute-start.40 = (bf16[96,320]{1,0:T(8,128)(2,1)S(1)}, bf16[96,320]{1,0:T(8,128)(2,1)S(1)}, u32[]{:S(2)}, u32[]{:S(2)}) collective-permute-start(bf16[96,320]{1,0:T(8,128)(2,1)S(1)} %get-tuple-element.166), channel_id=1, source_target_pairs={{0,2},{1,3},{2,4},{3,5},{4,6},{5,7},{6,0},{7,1},{8,10},{9,11},{10,... | collective-permute-start | bytes 184328 | tf_op jit(solution)/shard_map/ppermute | solution.py:58
  (47 other events, 370.2 us)
where the time goes:
time: 228 us
  Pallas kernels  129 us (57%)
  starting transfers between devices  52.5 us (23%)
  waiting for transfers between devices  33.1 us (15%)
  local copies, waits for them, and re-layouts  7.9 us (3%)
  other arithmetic  3.81 us (2%)
    ppermute x40, starting transfers between devices, send(): return lax.ppermute(value, ('seq', 'batch'), pairs)  40.8 us
    pallas_call x1, Pallas kernels, stage_two(): pl.pallas_call(functools.partial(stage_two_kernel, grid, order, taps), ou...  36.3 us
    ppermute x40, waiting for transfers between devices, send(): return lax.ppermute(value, ('seq', 'batch'), pairs)  33.1 us
    pallas_call x2, Pallas kernels, stage_four(): pl.pallas_call(functools.partial(stage_four_kernel, grid, order, begin, l...  23.8 us
    pallas_call x1, Pallas kernels, inner(): pl.pallas_call(functools.partial(inner_kernel, grid, order, taps), out_sh...  23.4 us
    pallas_call x1, Pallas kernels, stage_one(): pl.pallas_call(functools.partial(stage_one_kernel, grid, order), out_shap...  15.9 us
    pallas_call x1, Pallas kernels, inner_back(): pl.pallas_call(inner_back_kernel, out_shape=sds((count, span, hidden), F3...  14.8 us
    pallas_call x1, Pallas kernels, stage_three(): pl.pallas_call(stage_three_kernel, out_shape=(sds((count, span, hidden),...  9.58 us
  transfers between devices with their start and end apart: 44, of which 15 were waited for; matrix products, arithmetic and copies ran while one was open for 3% of the time, Pallas kernels for 40%

commit v1 on v0

--- a/solution.py
+++ b/solution.py
@@ -383,19 +383,21 @@
     )(*terms)
 
 
-def unpack_first_kernel(order, *refs):
-    terms, (down, tail) = refs[:-2], refs[-2:]
+def unpack_first_kernel(order, count, *refs):
+    terms, down, vectors = refs[:count], refs[count], refs[count + 1 :]
     hb = order.hb
     total = add_up([term[...] for term in terms], F32)
     down[...] = total[0:hb]
-    tail[...] = total[hb : hb + 16]
-
-
-def unpack_first(order, terms):
+    for row, vector in enumerate(vectors):
+        width = vector.shape[0]
+        vector[...] = total[hb + row : hb + row + 1, 0:width].reshape(width)
+
+
+def unpack_first(order, terms, widths):
     dl = terms[0].shape[1]
     return pl.pallas_call(
-        functools.partial(unpack_first_kernel, order),
-        out_shape=(sds((order.hb, dl), F32), sds((16, dl), F32)),
+        functools.partial(unpack_first_kernel, order, len(terms)),
+        out_shape=(sds((order.hb, dl), F32), *[sds((width,), F32) for width in widths]),
         compiler_params=pltpu.CompilerParams(vmem_limit_bytes=16 * MIB),
         cost_estimate=cost(0, 8 * dl * order.hb),
         name="unpack_first",
@@ -406,7 +408,7 @@
     grid, order, place, start_ref, length_ref, tokens, *refs
 ):
     parts, refs = refs[: 4 * grid.side], refs[4 * grid.side :]
-    hidden_one, narrow, conv_input, down_t, table, stage, sems = refs
+    hidden_one, narrow, conv_input, head, foot, down_t, table, stage, sems = refs
     model = tokens.shape[2]
     hidden = narrow.shape[2]
     hb, dl = order.hb, model // grid.seq
@@ -443,9 +445,12 @@
     active = gelu(scaled(unit, vec("middle_gain", hidden), vec("middle_shift", hidden)))
     valid = valid_rows(start_ref, length_ref, group, span)
     conv_input[...] = (active * valid).astype(BF).reshape(group, span, hidden)
-
-
-def stage_one(grid, order, place, start, lengths, tokens, parts):
+    reach = head.shape[1]
+    head[...] = conv_input[:, 0:reach]
+    foot[...] = conv_input[:, span - reach : span]
+
+
+def stage_one(grid, order, reach, place, start, lengths, tokens, parts):
     count, span, model = tokens.shape
     hidden = order.hidden
     group = group_of(count)
@@ -456,6 +461,8 @@
             sds((count, span, model), BF),
             sds((count, span, hidden), F32),
             sds((count, span, hidden), BF),
+            sds((count, reach, hidden), BF),
+            sds((count, reach, hidden), BF),
             sds((hidden, model), BF),
             sds((TABLE_ROWS, model), F32),
         ),
@@ -468,6 +475,8 @@
                 rows_of((group, span, model)),
                 rows_of((group, span, hidden)),
                 rows_of((group, span, hidden)),
+                rows_of((group, reach, hidden)),
+                rows_of((group, reach, hidden)),
                 whole((hidden, model)),
                 whole((TABLE_ROWS, model)),
             ],
@@ -622,7 +631,7 @@
 def stage_two_kernel(
     grid, order, taps, place, tokens, cotangent, conv_input, left, right, part, error, table,
     conv_t, up_t,
-    output, conv_out_grad, sums, part_a, part_b, part_c, part_d,
+    output, conv_out_grad, head, foot, sums, part_a, part_b, part_c, part_d,
     padded, threes, edges, total, conv_total, pieces, out_sems,
 ):
     group, span, model = tokens.shape
@@ -669,6 +678,8 @@
     grad, product = back_rows(twice, gain, unit, inverse)
     grad = grad.astype(BF)
     conv_out_grad[...] = grad.reshape(group, span, hidden)
+    head[...] = conv_out_grad[:, 0:reach]
+    foot[...] = conv_out_grad[:, span - reach : span]
     add("final_gain", product, 0.5)
     add("final_shift", twice, 0.5)
     add("conv_bias", grad.astype(F32))
@@ -708,6 +719,8 @@
         out_shape=(
             sds((count, span, model), BF),
             sds((count, span, hidden), BF),
+            sds((count, reach, hidden), BF),
+            sds((count, reach, hidden), BF),
             sds((TABLE_ROWS, model), F32),
             *[sds(pieces, BF)] * 4,
         ),
@@ -729,6 +742,8 @@
             out_specs=[
                 rows_of((group, span, model)),
                 rows_of((group, span, hidden)),
+                rows_of((group, reach, hidden)),
+                rows_of((group, reach, hidden)),
                 whole((TABLE_ROWS, model)),
                 *[pl.BlockSpec(memory_space=pl.ANY)] * 4,
             ],
@@ -980,12 +995,10 @@
     )(place, *inputs)
 
 
-def halos(cells, reach):
+def halos(head, foot):
     count = lax.axis_size("seq")
-    left = lax.ppermute(
-        cells[:, cells.shape[1] - reach :], "seq", [(i, i + 1) for i in range(count - 1)]
-    )
-    right = lax.ppermute(cells[:, :reach], "seq", [(i + 1, i) for i in range(count - 1)])
+    left = lax.ppermute(foot, "seq", [(i, i + 1) for i in range(count - 1)])
+    right = lax.ppermute(head, "seq", [(i + 1, i) for i in range(count - 1)])
     return left, right
 
 
@@ -1050,8 +1063,9 @@
         return found
 
     first = grid.gather_deep(first_piece)
-    neighbour, second_piece = lax.optimization_barrier((first[1], second_piece))
-    first[1] = neighbour
+    (first[1], second_piece), (place, start, lengths) = meet(
+        (first[1], second_piece), (place, start, lengths)
+    )
     second = grid.halves(grid.gather_deep(second_piece))
     one, two = grid.gather_near(*grid.halves(first))
     far_one, far_two = grid.gather_far(one, two)
@@ -1062,25 +1076,25 @@
     near, first = meet(near, first)
     near_other = grid.gather_core(near)
     far_one, far_two = grid.gather_far(*near)
-    hidden_one, narrow, conv_input, down_t, table = stage_one(
-        grid, order, place, start, lengths, tokens, first
-    )
-    far_one, far_two, near_other, (conv_input,) = meet(
-        far_one, far_two, near_other, (conv_input,)
-    )
-    left, right = halos(conv_input, reach)
+    hidden_one, narrow, conv_input, head, foot, down_t, table = stage_one(
+        grid, order, reach, place, start, lengths, tokens, first
+    )
+    far_one, far_two, near_other, (head, foot) = meet(
+        far_one, far_two, near_other, (head, foot)
+    )
+    left, right = halos(head, foot)
     far_one_other, far_two_other = grid.gather_core(far_one), grid.gather_core(far_two)
     second = [near[0], *far_one, near[1], *far_two]
     second += [near_other[0], *far_one_other, near_other[1], *far_two_other]
     part, error, conv_t, up_t = inner(
         grid, order, taps, reach, place, cotangent, conv_input, second
     )
-    block_output, conv_out_grad, sums, *rest = stage_two(
+    block_output, conv_out_grad, head, foot, sums, *rest = stage_two(
         grid, order, taps, place, tokens, cotangent, conv_input, left, right, part, error, table,
         conv_t, up_t,
     )
 
-    left, right = halos(conv_out_grad, reach)
+    left, right = halos(head, foot)
     rest = grid.reduce_core(*rest)
     part = inner_back(conv_out_grad, conv_t, reach)
     rest, (sums, left, right, part) = meet(rest, (sums, left, right, part))
@@ -1110,8 +1124,9 @@
     down = grid.reduce_near(*down)
     down = grid.reduce_deep(*down)
     conv_grad, up_grad = unpack_rest(order, taps, fold, rest)
-    down_grad, tail = unpack_first(order, down)
-    grads = {name: tail[ROW[name], : vectors[name].shape[0]] for name in vectors}
+    names = WIDE + NARROW
+    down_grad, *found = unpack_first(order, down, [vectors[name].shape[0] for name in names])
+    grads = dict(zip(names, found))
     return (
         block_output.reshape(shape),
         tokens_grad.reshape(shape),

time: 228 us -> 226 us (level)
  local copies, waits for them, and re-layouts: 7.9 us -> 3.48 us
  waiting for transfers between devices: 33.1 us -> 35.8 us
    slice x3 -> x0, local copies, waits for them, and re-layouts: 2.84 us -> none  [the longest x2 2.27 us: halos(): cells[:, :reach]]
  transfers between devices with their start and end apart: 44 -> 44, of which waited for: 15 -> 17; matrix products, arithmetic and copies ran while one was open for 3% -> 2% of each run, Pallas kernels for 40% -> 40%
where the time goes in v1:
time: 226 us
  Pallas kernels  130 us (58%)
  starting transfers between devices  51.7 us (23%)
  waiting for transfers between devices  35.8 us (16%)
  other arithmetic  3.77 us (2%)
  local copies, waits for them, and re-layouts  3.48 us (2%)
    ppermute x40, starting transfers between devices, send(): return lax.ppermute(value, ('seq', 'batch'), pairs)  41.7 us
    pallas_call x1, Pallas kernels, stage_two(): pl.pallas_call(functools.partial(stage_two_kernel, grid, order, taps), ou...  36.5 us
    ppermute x40, waiting for transfers between devices, send(): return lax.ppermute(value, ('seq', 'batch'), pairs)  34.7 us
    pallas_call x2, Pallas kernels, stage_four(): pl.pallas_call(functools.partial(stage_four_kernel, grid, order, begin, l...  23.8 us
    pallas_call x1, Pallas kernels, inner(): pl.pallas_call(functools.partial(inner_kernel, grid, order, taps), out_sh...  23.4 us
    pallas_call x1, Pallas kernels, stage_one(): pl.pallas_call(functools.partial(stage_one_kernel, grid, order), out_shap...  16.5 us
    pallas_call x1, Pallas kernels, inner_back(): pl.pallas_call(inner_back_kernel, out_shape=sds((count, span, hidden), F3...  14.8 us
    pallas_call x1, Pallas kernels, stage_three(): pl.pallas_call(stage_three_kernel, out_shape=(sds((count, span, hidden),...  9.58 us
  transfers between devices with their start and end apart: 44, of which 17 were waited for; matrix products, arithmetic and copies ran while one was open for 2% of the time, Pallas kernels for 40%

profile of v1, /device:TPU:0, one launch (start us, length us, event | category | flops | bytes accessed | tf_op | source)
XLA Modules:
  0.0 226.0 jit_solution(13567736861967680299)
XLA Ops:
  2.2 5.0 %collective-permute-start.4 = (bf16[96,320]{1,0:T(8,128)(2,1)}, bf16[96,320]{1,0:T(8,128)(2,1)S(1)}, u32[]{:S(2)}, u32[]{:S(2)}) collective-permute-start(bf16[96,320]{1,0:T(8,128)(2,1)} %pack_first.1), channel_id=1, source_target_pairs={{0,6},{1,7},{2,0},{3,1},{4,2},{5,3},{6,4},{7,5},{8,14},{9,15},{10,... | collective-permute-start | bytes 184328 | tf_op jit(solution)/shard_map/ppermute | solution.py:58
  9.5 2.0 pack_second.1
  20.5 2.0 collective-permute-start.7
  24.9 11.3 %collective-permute-done.8 = bf16[80,1120]{1,0:T(8,128)(2,1)S(1)} collective-permute-done((bf16[80,1120]{1,0:T(8,128)(2,1)}, bf16[80,1120]{1,0:T(8,128)(2,1)S(1)}, u32[]{:S(2)}, u32[]{:S(2)}) %collective-permute-start.8) | collective-permute-done | bytes 179232 | tf_op jit(solution)/shard_map/ppermute | solution.py:58
  37.9 7.1 %collective-permute-done.10 = bf16[2,80,1120]{2,1,0:T(8,128)(2,1)S(1)} collective-permute-done((bf16[2,80,1120]{2,1,0:T(8,128)(2,1)S(1)}, bf16[2,80,1120]{2,1,0:T(8,128)(2,1)S(1)}, u32[]{:S(2)}, u32[]{:S(2)}) %collective-permute-start.10) | collective-permute-done | bytes 358432 | tf_op jit(solution)/shard_map/ppermute | solution.py:58
  47.9 16.5 %stage_one.1 = (bf16[8,256,1280]{2,1,0:T(8,128)(2,1)}, f32[8,256,640]{2,1,0:T(8,128)}, bf16[8,256,640]{2,1,0:T(8,128)(2,1)}, bf16[8,32,640]{2,1,0:T(8,128)(2,1)}...) custom-call(s32[4]{0:T(128)} %pad_add_fusion.place, s32[1]{0:T(128)} %bitcast.5.start_ref, ...), custom_call_target="tpu_custom_call" | custom-call | flops 3355443200 | bytes 18350080 | tf_op jit(solution)/shard_map/stage_one/pallas_call | solution.py:458
  66.7 2.4 %collective-permute-start.20 = (bf16[8,32,640]{2,1,0:T(8,128)(2,1)}, bf16[8,32,640]{2,1,0:T(8,128)(2,1)S(1)}, u32[]{:S(2)}, u32[]{:S(2)}) collective-permute-start(bf16[8,32,640]{2,1,0:T(8,128)(2,1)} %get-tuple-element.127), channel_id=1, source_target_pairs={{0,8},{8,16},{16,24},{1,9},{9,17},{17,25},{2,10},{10,18},{18,26},{... | collective-permute-start | bytes 983048 | tf_op jit(solution)/shard_map/ppermute | solution.py:1000
  71.6 23.4 %inner.1 = (f32[8,256,640]{2,1,0:T(8,128)}, f32[8,256,640]{2,1,0:T(8,128)}, bf16[5,640,640]{2,1,0:T(8,128)(2,1)}, bf16[1280,640]{1,0:T(8,128)(2,1)}) custom-call(s32[4]{0:T(128)} %pad_add_fusion.place, bf16[8,256,1280]{2,1,0:T(8,128)(2,1)} %bitcast.93, bf16[8,256,640]{2,1,0:T(8,128)(2,1)} %get-tuple-element.122.conv_input, ...), custom_call_target="tpu_custom_call" | custom-call | flops 11744051200 | bytes 18350080 | tf_op jit(solution)/shard_map/inner/pallas_call | solution.py:594
  95.8 36.5 %stage_two.1 = (bf16[8,256,1280]{2,1,0:T(8,128)(2,1)}, bf16[8,256,640]{2,1,0:T(8,128)(2,1)}, bf16[8,32,640]{2,1,0:T(8,128)(2,1)}, bf16[8,32,640]{2,1,0:T(8,128)(...) custom-call(s32[4]{0:T(128)} %pad_add_fusion.place, ...), custom_call_target="tpu_custom_call" | custom-call | flops 15099494400 | bytes 31457280 | tf_op jit(solution)/shard_map/stage_two/pallas_call | solution.py:717
  132.4 5.0 %collective-permute-start.26 = (bf16[8,32,640]{2,1,0:T(8,128)(2,1)}, bf16[8,32,640]{2,1,0:T(8,128)(2,1)S(1)}, u32[]{:S(2)}, u32[]{:S(2)}) collective-permute-start(bf16[8,32,640]{2,1,0:T(8,128)(2,1)} %get-tuple-element.144), channel_id=1, source_target_pairs={{0,8},{8,16},{16,24},{1,9},{9,17},{17,25},{2,10},{10,18},{18,26},{... | collective-permute-start | bytes 983048 | tf_op jit(solution)/shard_map/ppermute | solution.py:1000
  139.0 14.8 %inner_back.1.part = f32[8,256,640]{2,1,0:T(8,128)} custom-call(bf16[8,256,640]{2,1,0:T(8,128)(2,1)} %get-tuple-element.146.conv_out_grad, bf16[5,640,640]{2,1,0:T(8,128)(2,1)} %get-tuple-element.136.conv_t), custom_call_target="tpu_custom_call" | custom-call | flops 8388608000 | bytes 7864320 | tf_op jit(solution)/shard_map/inner_back/pallas_call | solution.py:792
  155.6 2.6 %collective-permute-start.29 = (bf16[2,2,80,1120]{3,2,1,0:T(8,128)(2,1)S(1)}, bf16[2,2,80,1120]{3,2,1,0:T(8,128)(2,1)S(1)}, u32[]{:S(2)}, u32[]{:S(2)}) collective-permute-start(bf16[2,2,80,1120]{3,2,1,0:T(8,128)(2,1)S(1)} %slice_bitcast_fusion), channel_id=1, source_target_pairs={{0,8},{1,9},{2,10},{3,11},{4,12},{5,13},{6,14},{7,15},{8,0},{9,1},... | collective-permute-start | bytes 2150408 | tf_op jit(solution)/shard_map/ppermute | solution.py:58
  159.7 9.6 %stage_three.1 = (bf16[8,256,640]{2,1,0:T(8,128)(2,1)S(1)}, f32[16,1280]{1,0:T(8,128)S(1)}) custom-call(s32[1]{0:T(128)} %bitcast.5.start_ref, s32[8]{0:T(128)S(1)} %copy-done.7, f32[8,256,640]{2,1,0:T(8,128)S(1)} %copy-done.2, f32[8,256,640]{2,1,0:T(8,128)} %get-tuple-element.148.narrow, bf16[8,32,640]{2,1,0:T(8,128)(2,1)S(1)} %collective-permute-done.26.left, ...), custom_call_target="tpu_custom_call" | custom-call | flops 1677721600 | bytes 13107200 | tf_op jit(solution)/shard_map/stage_three/pallas_call | solution.py:850
  169.3 9.5 %stage_four.2 = (bf16[8,256,1280]{2,1,0:T(8,128)(2,1)}, f32[16,1280]{1,0:T(8,128)S(1)}) custom-call(s32[4]{0:T(128)S(1)} %copy-done.6, bf16[8,256,1280]{2,1,0:T(8,128)(2,1)} %bitcast.91, bf16[8,256,1280]{2,1,0:T(8,128)(2,1)} %bitcast.95, bf16[8,256,640]{2,1,0:T(8,128)(2,1)S(1)} %get-tuple-element.152.narrow_grad.refs_1_, f32[16,1280]{1,0:T(8,128)S(1)} %copy-done.4, ...), custom_call_target="tpu_custom_call" | custom-call | flops 3355443200 | bytes 11796480 | tf_op jit(solution)/shard_map/stage_four/pallas_call | solution.py:979
  179.2 2.8 %collective-permute-start.31 = (bf16[2,80,1120]{2,1,0:T(8,128)(2,1)S(1)}, bf16[2,80,1120]{2,1,0:T(8,128)(2,1)S(1)}, u32[]{:S(2)}, u32[]{:S(2)}) collective-permute-start(bf16[2,80,1120]{2,1,0:T(8,128)(2,1)S(1)} %slice_bitcast_fusion.2), channel_id=1, source_target_pairs={{0,16},{1,17},{2,18},{3,19},{4,20},{5,21},{6,22},{7,23},{8,24},{9,... | collective-permute-start | bytes 1075208 | tf_op jit(solution)/shard_map/ppermute | solution.py:58
  182.1 14.3 %stage_four.3 = (bf16[8,256,1280]{2,1,0:T(8,128)(2,1)}, f32[16,1280]{1,0:T(8,128)}, bf16[2,2,2,96,320]{4,3,2,1,0:T(8,128)(2,1)S(1)}, bf16[2,2,2,96,320]{4,3,2,1,...) custom-call(s32[4]{0:T(128)S(1)} %copy-done.6, ...), custom_call_target="tpu_custom_call", output_to_operand_aliasing={{0}: (9, {})} | custom-call | flops 3355443200 | bytes 11796480 | tf_op jit(solution)/shard_map/stage_four/pallas_call | solution.py:979
  200.1 2.1 collective-permute-start.37
  202.2 1.9 collective-permute-start.43
  204.1 3.2 %collective-permute-start.42 = (bf16[80,1120]{1,0:T(8,128)(2,1)S(1)}, bf16[80,1120]{1,0:T(8,128)(2,1)S(1)}, u32[]{:S(2)}, u32[]{:S(2)}) collective-permute-start(bf16[80,1120]{1,0:T(8,128)(2,1)S(1)} %get-tuple-element.191), channel_id=1, source_target_pairs={{0,4},{1,5},{2,6},{3,7},{4,0},{5,1},{6,2},{7,3},{8,12},{9,13},{10,... | collective-permute-start | bytes 537608 | tf_op jit(solution)/shard_map/ppermute | solution.py:58
  207.3 2.0 collective-permute-done.37
  211.4 3.2 %collective-permute-done.38 = bf16[2,96,320]{2,1,0:T(8,128)(2,1)S(1)} collective-permute-done((bf16[2,96,320]{2,1,0:T(8,128)(2,1)S(1)}, bf16[2,96,320]{2,1,0:T(8,128)(2,1)S(1)}, u32[]{:S(2)}, u32[]{:S(2)}) %collective-permute-start.38) | collective-permute-done | bytes 122912 | tf_op jit(solution)/shard_map/ppermute | solution.py:58
  214.7 1.8 collective-permute-start.40
  216.5 3.2 %collective-permute-start.39 = (bf16[96,320]{1,0:T(8,128)(2,1)S(1)}, bf16[96,320]{1,0:T(8,128)(2,1)S(1)}, u32[]{:S(2)}, u32[]{:S(2)}) collective-permute-start(bf16[96,320]{1,0:T(8,128)(2,1)S(1)} %get-tuple-element.195), channel_id=1, source_target_pairs={{0,4},{1,5},{2,6},{3,7},{4,0},{5,1},{6,2},{7,3},{8,12},{9,13},{10,... | collective-permute-start | bytes 184328 | tf_op jit(solution)/shard_map/ppermute | solution.py:58
  221.2 2.6 %collective-permute-done.42.refs_2_ = bf16[80,1120]{1,0:T(8,128)(2,1)S(1)} collective-permute-done((bf16[80,1120]{1,0:T(8,128)(2,1)S(1)}, bf16[80,1120]{1,0:T(8,128)(2,1)S(1)}, u32[]{:S(2)}, u32[]{:S(2)}) %collective-permute-start.42) | collective-permute-done | bytes 179232 | tf_op jit(solution)/shard_map/ppermute | solution.py:58
  (165 shorter events, 40.0 us)
Async XLA Ops:
  2.2 14.0 %collective-permute-start.4 = (bf16[96,320]{1,0:T(8,128)(2,1)}, bf16[96,320]{1,0:T(8,128)(2,1)S(1)}, u32[]{:S(2)}, u32[]{:S(2)}) collective-permute-start(bf16[96,320]{1,0:T(8,128)(2,1)} %pack_first.1), channel_id=1, source_target_pairs={{0,6},{1,7},{2,0},{3,1},{4,2},{5,3},{6,4},{7,5},{8,14},{9,15},{10,... | collective-permute-start | bytes 184328 | tf_op jit(solution)/shard_map/ppermute | solution.py:58
  19.4 16.7 %collective-permute-start.8 = (bf16[80,1120]{1,0:T(8,128)(2,1)}, bf16[80,1120]{1,0:T(8,128)(2,1)S(1)}, u32[]{:S(2)}, u32[]{:S(2)}) collective-permute-start(bf16[80,1120]{1,0:T(8,128)(2,1)} %pack_second.1), channel_id=1, source_target_pairs={{0,4},{1,5},{2,6},{3,7},{4,0},{5,1},{6,2},{7,3},{8,12},{9,13},{10,... | collective-permute-start | bytes 537608 | tf_op jit(solution)/shard_map/ppermute | solution.py:58
  20.5 15.7 %collective-permute-start.7 = (bf16[80,1120]{1,0:T(8,128)(2,1)}, bf16[80,1120]{1,0:T(8,128)(2,1)S(1)}, u32[]{:S(2)}, u32[]{:S(2)}) collective-permute-start(bf16[80,1120]{1,0:T(8,128)(2,1)} %pack_second.1), channel_id=1, source_target_pairs={{0,2},{1,3},{2,4},{3,5},{4,6},{5,7},{6,0},{7,1},{8,10},{9,11},{10,... | collective-permute-start | bytes 537608 | tf_op jit(solution)/shard_map/ppermute | solution.py:58
  22.6 13.7 %collective-permute-start.2 = (bf16[2,2,96,320]{3,2,1,0:T(8,128)(2,1)S(1)}, bf16[2,2,96,320]{3,2,1,0:T(8,128)(2,1)S(1)}, u32[]{:S(2)}, u32[]{:S(2)}) collective-permute-start(bf16[2,2,96,320]{3,2,1,0:T(8,128)(2,1)S(1)} %pad_maximum_fusion.4.refs_0_), channel_id=1, source_target_pairs={{0,16},{1,17},{2,18},{3,19},{4,20},{5,21},{6,22},{7,23},{8,24},{9,... | collective-permute-start | bytes 737288 | tf_op jit(solution)/shard_map/ppermute | solution.py:58
  23.2 13.1 %collective-permute-start.6 = (bf16[2,2,96,320]{3,2,1,0:T(8,128)(2,1)S(1)}, bf16[2,2,96,320]{3,2,1,0:T(8,128)(2,1)S(1)}, u32[]{:S(2)}, u32[]{:S(2)}) collective-permute-start(bf16[2,2,96,320]{3,2,1,0:T(8,128)(2,1)S(1)} %pad_maximum_fusion.5.refs_2_), channel_id=1, source_target_pairs={{0,8},{1,9},{2,10},{3,11},{4,12},{5,13},{6,14},{7,15},{8,0},{9,1},... | collective-permute-start | bytes 737288 | tf_op jit(solution)/shard_map/ppermute | solution.py:58
  46.6 17.9 %collective-permute-start.18 = (bf16[2,2,80,1120]{3,2,1,0:T(8,128)(2,1)S(1)}, bf16[2,2,80,1120]{3,2,1,0:T(8,128)(2,1)S(1)}, u32[]{:S(2)}, u32[]{:S(2)}) collective-permute-start(bf16[2,2,80,1120]{3,2,1,0:T(8,128)(2,1)S(1)} %pad_maximum_fusion.refs_0_), channel_id=1, source_target_pairs={{0,1},{1,0},{2,3},{3,2},{4,5},{5,4},{6,7},{7,6},{8,9},{9,8},{10,11... | collective-permute-start | bytes 2150408 | tf_op jit(solution)/shard_map/ppermute | solution.py:58
  46.8 18.8 %collective-permute-start.16 = (bf16[2,2,80,1120]{3,2,1,0:T(8,128)(2,1)S(1)}, bf16[2,2,80,1120]{3,2,1,0:T(8,128)(2,1)S(1)}, u32[]{:S(2)}, u32[]{:S(2)}) collective-permute-start(bf16[2,2,80,1120]{3,2,1,0:T(8,128)(2,1)S(1)} %pad_maximum_fusion.refs_0_), channel_id=1, source_target_pairs={{0,16},{1,17},{2,18},{3,19},{4,20},{5,21},{6,22},{7,23},{8,24},{9,... | collective-permute-start | bytes 2150408 | tf_op jit(solution)/shard_map/ppermute | solution.py:58
  47.3 18.3 %collective-permute-start.19 = (bf16[2,2,80,1120]{3,2,1,0:T(8,128)(2,1)S(1)}, bf16[2,2,80,1120]{3,2,1,0:T(8,128)(2,1)S(1)}, u32[]{:S(2)}, u32[]{:S(2)}) collective-permute-start(bf16[2,2,80,1120]{3,2,1,0:T(8,128)(2,1)S(1)} %pad_maximum_fusion.1.refs_2_), channel_id=1, source_target_pairs={{0,1},{1,0},{2,3},{3,2},{4,5},{5,4},{6,7},{7,6},{8,9},{9,8},{10,11... | collective-permute-start | bytes 2150408 | tf_op jit(solution)/shard_map/ppermute | solution.py:58
  47.4 18.8 %collective-permute-start.17 = (bf16[2,2,80,1120]{3,2,1,0:T(8,128)(2,1)S(1)}, bf16[2,2,80,1120]{3,2,1,0:T(8,128)(2,1)S(1)}, u32[]{:S(2)}, u32[]{:S(2)}) collective-permute-start(bf16[2,2,80,1120]{3,2,1,0:T(8,128)(2,1)S(1)} %pad_maximum_fusion.1.refs_2_), channel_id=1, source_target_pairs={{0,8},{1,9},{2,10},{3,11},{4,12},{5,13},{6,14},{7,15},{8,0},{9,1},... | collective-permute-start | bytes 2150408 | tf_op jit(solution)/shard_map/ppermute | solution.py:58
  66.7 28.3 %collective-permute-start.20 = (bf16[8,32,640]{2,1,0:T(8,128)(2,1)}, bf16[8,32,640]{2,1,0:T(8,128)(2,1)S(1)}, u32[]{:S(2)}, u32[]{:S(2)}) collective-permute-start(bf16[8,32,640]{2,1,0:T(8,128)(2,1)} %get-tuple-element.127), channel_id=1, source_target_pairs={{0,8},{8,16},{16,24},{1,9},{9,17},{17,25},{2,10},{10,18},{18,26},{... | collective-permute-start | bytes 983048 | tf_op jit(solution)/shard_map/ppermute | solution.py:1000
  69.2 25.9 %collective-permute-start.21 = (bf16[8,32,640]{2,1,0:T(8,128)(2,1)}, bf16[8,32,640]{2,1,0:T(8,128)(2,1)}, u32[]{:S(2)}, u32[]{:S(2)}) collective-permute-start(bf16[8,32,640]{2,1,0:T(8,128)(2,1)} %get-tuple-element.128), channel_id=1, source_target_pairs={{8,0},{16,8},{24,16},{9,1},{17,9},{25,17},{10,2},{18,10},{26,18},{... | collective-permute-start | bytes 983048 | tf_op jit(solution)/shard_map/ppermute | solution.py:1001
  132.3 21.4 %collective-permute-start.24 = (bf16[2,2,2,80,1120]{4,3,2,1,0:T(8,128)(2,1)}, bf16[2,2,2,80,1120]{4,3,2,1,0:T(8,128)(2,1)S(1)}, u32[]{:S(2)}, u32[]{:S(2)}) collective-permute-start(bf16[2,2,2,80,1120]{4,3,2,1,0:T(8,128)(2,1)} %get-tuple-element.140), channel_id=1, source_target_pairs={{0,1},{1,0},{2,3},{3,2},{4,5},{5,4},{6,7},{7,6},{8,9},{9,8},{10,11... | collective-permute-start | bytes 4300808 | tf_op jit(solution)/shard_map/ppermute | solution.py:58
  132.4 22.1 %collective-permute-start.26 = (bf16[8,32,640]{2,1,0:T(8,128)(2,1)}, bf16[8,32,640]{2,1,0:T(8,128)(2,1)S(1)}, u32[]{:S(2)}, u32[]{:S(2)}) collective-permute-start(bf16[8,32,640]{2,1,0:T(8,128)(2,1)} %get-tuple-element.144), channel_id=1, source_target_pairs={{0,8},{8,16},{16,24},{1,9},{9,17},{17,25},{2,10},{10,18},{18,26},{... | collective-permute-start | bytes 983048 | tf_op jit(solution)/shard_map/ppermute | solution.py:1000
  137.4 18.2 %collective-permute-start.27 = (bf16[8,32,640]{2,1,0:T(8,128)(2,1)}, bf16[8,32,640]{2,1,0:T(8,128)(2,1)S(1)}, u32[]{:S(2)}, u32[]{:S(2)}) collective-permute-start(bf16[8,32,640]{2,1,0:T(8,128)(2,1)} %get-tuple-element.145), channel_id=1, source_target_pairs={{8,0},{16,8},{24,16},{9,1},{17,9},{25,17},{10,2},{18,10},{26,18},{... | collective-permute-start | bytes 983048 | tf_op jit(solution)/shard_map/ppermute | solution.py:1001
  138.7 15.4 %collective-permute-start.25 = (bf16[2,2,2,80,1120]{4,3,2,1,0:T(8,128)(2,1)}, bf16[2,2,2,80,1120]{4,3,2,1,0:T(8,128)(2,1)S(1)}, u32[]{:S(2)}, u32[]{:S(2)}) collective-permute-start(bf16[2,2,2,80,1120]{4,3,2,1,0:T(8,128)(2,1)} %get-tuple-element.142), channel_id=1, source_target_pairs={{0,1},{1,0},{2,3},{3,2},{4,5},{5,4},{6,7},{7,6},{8,9},{9,8},{10,11... | collective-permute-start | bytes 4300808 | tf_op jit(solution)/shard_map/ppermute | solution.py:58
  155.6 23.2 %collective-permute-start.29 = (bf16[2,2,80,1120]{3,2,1,0:T(8,128)(2,1)S(1)}, bf16[2,2,80,1120]{3,2,1,0:T(8,128)(2,1)S(1)}, u32[]{:S(2)}, u32[]{:S(2)}) collective-permute-start(bf16[2,2,80,1120]{3,2,1,0:T(8,128)(2,1)S(1)} %slice_bitcast_fusion), channel_id=1, source_target_pairs={{0,8},{1,9},{2,10},{3,11},{4,12},{5,13},{6,14},{7,15},{8,0},{9,1},... | collective-permute-start | bytes 2150408 | tf_op jit(solution)/shard_map/ppermute | solution.py:58
  158.3 20.7 %collective-permute-start.28 = (bf16[2,2,80,1120]{3,2,1,0:T(8,128)(2,1)S(1)}, bf16[2,2,80,1120]{3,2,1,0:T(8,128)(2,1)S(1)}, u32[]{:S(2)}, u32[]{:S(2)}) collective-permute-start(bf16[2,2,80,1120]{3,2,1,0:T(8,128)(2,1)S(1)} %slice_bitcast_fusion.1), channel_id=1, source_target_pairs={{0,16},{1,17},{2,18},{3,19},{4,20},{5,21},{6,22},{7,23},{8,24},{9,... | collective-permute-start | bytes 2150408 | tf_op jit(solution)/shard_map/ppermute | solution.py:58
  179.2 17.2 %collective-permute-start.31 = (bf16[2,80,1120]{2,1,0:T(8,128)(2,1)S(1)}, bf16[2,80,1120]{2,1,0:T(8,128)(2,1)S(1)}, u32[]{:S(2)}, u32[]{:S(2)}) collective-permute-start(bf16[2,80,1120]{2,1,0:T(8,128)(2,1)S(1)} %slice_bitcast_fusion.2), channel_id=1, source_target_pairs={{0,16},{1,17},{2,18},{3,19},{4,20},{5,21},{6,22},{7,23},{8,24},{9,... | collective-permute-start | bytes 1075208 | tf_op jit(solution)/shard_map/ppermute | solution.py:58
  182.0 14.5 %collective-permute-start.30 = (bf16[2,80,1120]{2,1,0:T(8,128)(2,1)S(1)}, bf16[2,80,1120]{2,1,0:T(8,128)(2,1)S(1)}, u32[]{:S(2)}, u32[]{:S(2)}) collective-permute-start(bf16[2,80,1120]{2,1,0:T(8,128)(2,1)S(1)} %slice_bitcast_fusion.3), channel_id=1, source_target_pairs={{0,8},{1,9},{2,10},{3,11},{4,12},{5,13},{6,14},{7,15},{8,0},{9,1},... | collective-permute-start | bytes 1075208 | tf_op jit(solution)/shard_map/ppermute | solution.py:58
  199.8 19.9 %collective-permute-start.41 = (bf16[80,1120]{1,0:T(8,128)(2,1)S(1)}, bf16[80,1120]{1,0:T(8,128)(2,1)S(1)}, u32[]{:S(2)}, u32[]{:S(2)}) collective-permute-start(bf16[80,1120]{1,0:T(8,128)(2,1)S(1)} %get-tuple-element.192), channel_id=1, source_target_pairs={{0,6},{1,7},{2,0},{3,1},{4,2},{5,3},{6,4},{7,5},{8,14},{9,15},{10,... | collective-permute-start | bytes 537608 | tf_op jit(solution)/shard_map/ppermute | solution.py:58
  200.1 9.2 %collective-permute-start.37 = (bf16[2,2,96,320]{3,2,1,0:T(8,128)(2,1)S(1)}, bf16[2,2,96,320]{3,2,1,0:T(8,128)(2,1)S(1)}, u32[]{:S(2)}, u32[]{:S(2)}) collective-permute-start(bf16[2,2,96,320]{3,2,1,0:T(8,128)(2,1)S(1)} %slice_bitcast_fusion.4), channel_id=1, source_target_pairs={{0,8},{1,9},{2,10},{3,11},{4,12},{5,13},{6,14},{7,15},{8,0},{9,1},... | collective-permute-start | bytes 737288 | tf_op jit(solution)/shard_map/ppermute | solution.py:58
  202.2 19.0 %collective-permute-start.43 = (bf16[80,1120]{1,0:T(8,128)(2,1)S(1)}, bf16[80,1120]{1,0:T(8,128)(2,1)S(1)}, u32[]{:S(2)}, u32[]{:S(2)}) collective-permute-start(bf16[80,1120]{1,0:T(8,128)(2,1)S(1)} %get-tuple-element.190), channel_id=1, source_target_pairs={{0,2},{1,3},{2,4},{3,5},{4,6},{5,7},{6,0},{7,1},{8,10},{9,11},{10,... | collective-permute-start | bytes 537608 | tf_op jit(solution)/shard_map/ppermute | solution.py:58
  204.1 19.7 %collective-permute-start.42 = (bf16[80,1120]{1,0:T(8,128)(2,1)S(1)}, bf16[80,1120]{1,0:T(8,128)(2,1)S(1)}, u32[]{:S(2)}, u32[]{:S(2)}) collective-permute-start(bf16[80,1120]{1,0:T(8,128)(2,1)S(1)} %get-tuple-element.191), channel_id=1, source_target_pairs={{0,4},{1,5},{2,6},{3,7},{4,0},{5,1},{6,2},{7,3},{8,12},{9,13},{10,... | collective-permute-start | bytes 537608 | tf_op jit(solution)/shard_map/ppermute | solution.py:58
  214.7 10.2 %collective-permute-start.40 = (bf16[96,320]{1,0:T(8,128)(2,1)S(1)}, bf16[96,320]{1,0:T(8,128)(2,1)S(1)}, u32[]{:S(2)}, u32[]{:S(2)}) collective-permute-start(bf16[96,320]{1,0:T(8,128)(2,1)S(1)} %get-tuple-element.194), channel_id=1, source_target_pairs={{0,2},{1,3},{2,4},{3,5},{4,6},{5,7},{6,0},{7,1},{8,10},{9,11},{10,... | collective-permute-start | bytes 184328 | tf_op jit(solution)/shard_map/ppermute | solution.py:58
  (48 other events, 366.4 us)

commit v2 on v1

--- a/solution.py
+++ b/solution.py
@@ -205,15 +205,29 @@
     return stage[(b % 2,) + spot_of(grid, place, s, b)]
 
 
-def hand_out(pieces, parts, sems):
-    copies = [
-        pltpu.make_async_copy(pieces.at[index // 2, index % 2], part, sems.at[index])
-        for index, part in enumerate(parts)
-    ]
-    for copy in copies:
-        copy.start()
-    for copy in copies:
-        copy.wait()
+def hand_out(place, parity, pieces, parts, sems):
+    def copies(core):
+        return [
+            pltpu.make_async_copy(
+                pieces.at[core, half], parts[2 * core + half], sems.at[2 * core + half]
+            )
+            for half in range(2)
+        ]
+
+    @pl.when(place[3] == parity)
+    def _():
+        for copy in copies(0):
+            copy.start()
+
+    @pl.when(place[3] != parity)
+    def _():
+        for copy in copies(1):
+            copy.start()
+
+    if parity == 1:
+        for core in range(2):
+            for copy in copies(core):
+                copy.wait()
 
 
 def piece_shape(grid, rows, lanes):
@@ -690,7 +704,7 @@
 
     @pl.when(step == pl.num_programs(0) - 1)
     def _():
-        for b in range(grid.batch):
+        for b in [*range(0, grid.batch, 2), *range(1, grid.batch, 2)]:
             for offset, spot, length in order.runs(b * hb, hb):
                 rows = [
                     conv_total[spot : spot + length, k * hidden : (k + 1) * hidden].astype(BF)
@@ -701,7 +715,8 @@
                     rows.append(total[at : at + length].astype(BF))
                 for s, piece in enumerate(wire_from_rows(order, rows)):
                     pieces[distance(grid, place, s, b) + (pl.ds(offset, length),)] = piece
-        hand_out(pieces, (part_a, part_b, part_c, part_d), out_sems)
+            if b >= grid.batch - 2:
+                hand_out(place, b % 2, pieces, (part_a, part_b, part_c, part_d), out_sems)
 
 
 def stage_two(
@@ -919,7 +934,7 @@
         def _():
             wide = model // grid.batch
             sub = lax.broadcasted_iota(jnp.int32, (TABLE_ROWS, dl), 0)
-            for b in range(grid.batch):
+            for b in [*range(0, grid.batch, 2), *range(1, grid.batch, 2)]:
                 upper = sums[:, b * wide : (b + 1) * wide]
                 runs = order.runs(b * hb, hb)
                 lower = join([sums[:, spot : spot + length] for _, spot, length in runs])
@@ -934,7 +949,8 @@
                             spot : spot + length, s * dl : (s + 1) * dl
                         ].astype(BF)
                     pieces[to + (pl.ds(hb, 16),)] = tail
-            hand_out(pieces, parts, out_sems)
+                if b >= grid.batch - 2:
+                    hand_out(place, b % 2, pieces, parts, out_sems)
 
 
 def stage_four(

time: 226 us -> 226 us (level)
  no operation moved by 1% of the time
where the time goes in v2:
time: 226 us
  Pallas kernels  130 us (58%)
  starting transfers between devices  51.8 us (23%)
  waiting for transfers between devices  35.7 us (16%)
  other arithmetic  3.77 us (2%)
  local copies, waits for them, and re-layouts  3.48 us (2%)
    ppermute x40, starting transfers between devices, send(): return lax.ppermute(value, ('seq', 'batch'), pairs)  41.8 us
    pallas_call x1, Pallas kernels, stage_two(): pl.pallas_call(functools.partial(stage_two_kernel, grid, order, taps), ou...  36.3 us
    ppermute x40, waiting for transfers between devices, send(): return lax.ppermute(value, ('seq', 'batch'), pairs)  34.7 us
    pallas_call x2, Pallas kernels, stage_four(): pl.pallas_call(functools.partial(stage_four_kernel, grid, order, begin, l...  23.9 us
    pallas_call x1, Pallas kernels, inner(): pl.pallas_call(functools.partial(inner_kernel, grid, order, taps), out_sh...  23.2 us
    pallas_call x1, Pallas kernels, stage_one(): pl.pallas_call(functools.partial(stage_one_kernel, grid, order), out_shap...  16.5 us
    pallas_call x1, Pallas kernels, inner_back(): pl.pallas_call(inner_back_kernel, out_shape=sds((count, span, hidden), F3...  14.9 us
    pallas_call x1, Pallas kernels, stage_three(): pl.pallas_call(stage_three_kernel, out_shape=(sds((count, span, hidden),...  9.58 us
  transfers between devices with their start and end apart: 44, of which 17 were waited for; matrix products, arithmetic and copies ran while one was open for 2% of the time, Pallas kernels for 40%

profile of v2, /device:TPU:0, one launch (start us, length us, event | category | flops | bytes accessed | tf_op | source)
XLA Modules:
  0.0 225.8 jit_solution(1182752573368774900)
XLA Ops:
  2.2 5.0 %collective-permute-start.4 = (bf16[96,320]{1,0:T(8,128)(2,1)}, bf16[96,320]{1,0:T(8,128)(2,1)S(1)}, u32[]{:S(2)}, u32[]{:S(2)}) collective-permute-start(bf16[96,320]{1,0:T(8,128)(2,1)} %pack_first.1), channel_id=1, source_target_pairs={{0,6},{1,7},{2,0},{3,1},{4,2},{5,3},{6,4},{7,5},{8,14},{9,15},{10,... | collective-permute-start | bytes 184328 | tf_op jit(solution)/shard_map/ppermute | solution.py:58
  9.5 2.0 pack_second.1
  20.5 2.0 collective-permute-start.7
  24.9 11.3 %collective-permute-done.8 = bf16[80,1120]{1,0:T(8,128)(2,1)S(1)} collective-permute-done((bf16[80,1120]{1,0:T(8,128)(2,1)}, bf16[80,1120]{1,0:T(8,128)(2,1)S(1)}, u32[]{:S(2)}, u32[]{:S(2)}) %collective-permute-start.8) | collective-permute-done | bytes 179232 | tf_op jit(solution)/shard_map/ppermute | solution.py:58
  37.9 7.1 %collective-permute-done.10 = bf16[2,80,1120]{2,1,0:T(8,128)(2,1)S(1)} collective-permute-done((bf16[2,80,1120]{2,1,0:T(8,128)(2,1)S(1)}, bf16[2,80,1120]{2,1,0:T(8,128)(2,1)S(1)}, u32[]{:S(2)}, u32[]{:S(2)}) %collective-permute-start.10) | collective-permute-done | bytes 358432 | tf_op jit(solution)/shard_map/ppermute | solution.py:58
  47.9 16.5 %stage_one.1 = (bf16[8,256,1280]{2,1,0:T(8,128)(2,1)}, f32[8,256,640]{2,1,0:T(8,128)}, bf16[8,256,640]{2,1,0:T(8,128)(2,1)}, bf16[8,32,640]{2,1,0:T(8,128)(2,1)}...) custom-call(s32[4]{0:T(128)} %pad_add_fusion.place, s32[1]{0:T(128)} %bitcast.5.start_ref, ...), custom_call_target="tpu_custom_call" | custom-call | flops 3355443200 | bytes 18350080 | tf_op jit(solution)/shard_map/stage_one/pallas_call | solution.py:472
  66.7 2.4 %collective-permute-start.20 = (bf16[8,32,640]{2,1,0:T(8,128)(2,1)}, bf16[8,32,640]{2,1,0:T(8,128)(2,1)S(1)}, u32[]{:S(2)}, u32[]{:S(2)}) collective-permute-start(bf16[8,32,640]{2,1,0:T(8,128)(2,1)} %get-tuple-element.127), channel_id=1, source_target_pairs={{0,8},{8,16},{16,24},{1,9},{9,17},{17,25},{2,10},{10,18},{18,26},{... | collective-permute-start | bytes 983048 | tf_op jit(solution)/shard_map/ppermute | solution.py:1016
  71.6 23.2 %inner.1 = (f32[8,256,640]{2,1,0:T(8,128)}, f32[8,256,640]{2,1,0:T(8,128)}, bf16[5,640,640]{2,1,0:T(8,128)(2,1)}, bf16[1280,640]{1,0:T(8,128)(2,1)}) custom-call(s32[4]{0:T(128)} %pad_add_fusion.place, bf16[8,256,1280]{2,1,0:T(8,128)(2,1)} %bitcast.93, bf16[8,256,640]{2,1,0:T(8,128)(2,1)} %get-tuple-element.122.conv_input, ...), custom_call_target="tpu_custom_call" | custom-call | flops 11744051200 | bytes 18350080 | tf_op jit(solution)/shard_map/inner/pallas_call | solution.py:608
  95.6 36.3 %stage_two.1 = (bf16[8,256,1280]{2,1,0:T(8,128)(2,1)}, bf16[8,256,640]{2,1,0:T(8,128)(2,1)}, bf16[8,32,640]{2,1,0:T(8,128)(2,1)}, bf16[8,32,640]{2,1,0:T(8,128)(...) custom-call(s32[4]{0:T(128)} %pad_add_fusion.place, ...), custom_call_target="tpu_custom_call" | custom-call | flops 15099494400 | bytes 31457280 | tf_op jit(solution)/shard_map/stage_two/pallas_call | solution.py:732
  131.9 5.0 %collective-permute-start.26 = (bf16[8,32,640]{2,1,0:T(8,128)(2,1)}, bf16[8,32,640]{2,1,0:T(8,128)(2,1)S(1)}, u32[]{:S(2)}, u32[]{:S(2)}) collective-permute-start(bf16[8,32,640]{2,1,0:T(8,128)(2,1)} %get-tuple-element.144), channel_id=1, source_target_pairs={{0,8},{8,16},{16,24},{1,9},{9,17},{17,25},{2,10},{10,18},{18,26},{... | collective-permute-start | bytes 983048 | tf_op jit(solution)/shard_map/ppermute | solution.py:1016
  138.5 14.9 %inner_back.1.part = f32[8,256,640]{2,1,0:T(8,128)} custom-call(bf16[8,256,640]{2,1,0:T(8,128)(2,1)} %get-tuple-element.146.conv_out_grad, bf16[5,640,640]{2,1,0:T(8,128)(2,1)} %get-tuple-element.136.conv_t), custom_call_target="tpu_custom_call" | custom-call | flops 8388608000 | bytes 7864320 | tf_op jit(solution)/shard_map/inner_back/pallas_call | solution.py:807
  155.2 2.7 %collective-permute-start.29 = (bf16[2,2,80,1120]{3,2,1,0:T(8,128)(2,1)S(1)}, bf16[2,2,80,1120]{3,2,1,0:T(8,128)(2,1)S(1)}, u32[]{:S(2)}, u32[]{:S(2)}) collective-permute-start(bf16[2,2,80,1120]{3,2,1,0:T(8,128)(2,1)S(1)} %slice_bitcast_fusion), channel_id=1, source_target_pairs={{0,8},{1,9},{2,10},{3,11},{4,12},{5,13},{6,14},{7,15},{8,0},{9,1},... | collective-permute-start | bytes 2150408 | tf_op jit(solution)/shard_map/ppermute | solution.py:58
  159.5 9.6 %stage_three.1 = (bf16[8,256,640]{2,1,0:T(8,128)(2,1)S(1)}, f32[16,1280]{1,0:T(8,128)S(1)}) custom-call(s32[1]{0:T(128)} %bitcast.5.start_ref, s32[8]{0:T(128)S(1)} %copy-done.7, f32[8,256,640]{2,1,0:T(8,128)S(1)} %copy-done.2, f32[8,256,640]{2,1,0:T(8,128)} %get-tuple-element.148.narrow, bf16[8,32,640]{2,1,0:T(8,128)(2,1)S(1)} %collective-permute-done.26.left, ...), custom_call_target="tpu_custom_call" | custom-call | flops 1677721600 | bytes 13107200 | tf_op jit(solution)/shard_map/stage_three/pallas_call | solution.py:865
  169.1 9.5 %stage_four.2 = (bf16[8,256,1280]{2,1,0:T(8,128)(2,1)}, f32[16,1280]{1,0:T(8,128)S(1)}) custom-call(s32[4]{0:T(128)S(1)} %copy-done.6, bf16[8,256,1280]{2,1,0:T(8,128)(2,1)} %bitcast.91, bf16[8,256,1280]{2,1,0:T(8,128)(2,1)} %bitcast.95, bf16[8,256,640]{2,1,0:T(8,128)(2,1)S(1)} %get-tuple-element.152.narrow_grad.refs_1_, f32[16,1280]{1,0:T(8,128)S(1)} %copy-done.4, ...), custom_call_target="tpu_custom_call" | custom-call | flops 3355443200 | bytes 11796480 | tf_op jit(solution)/shard_map/stage_four/pallas_call | solution.py:995
  179.0 2.8 %collective-permute-start.31 = (bf16[2,80,1120]{2,1,0:T(8,128)(2,1)S(1)}, bf16[2,80,1120]{2,1,0:T(8,128)(2,1)S(1)}, u32[]{:S(2)}, u32[]{:S(2)}) collective-permute-start(bf16[2,80,1120]{2,1,0:T(8,128)(2,1)S(1)} %slice_bitcast_fusion.2), channel_id=1, source_target_pairs={{0,16},{1,17},{2,18},{3,19},{4,20},{5,21},{6,22},{7,23},{8,24},{9,... | collective-permute-start | bytes 1075208 | tf_op jit(solution)/shard_map/ppermute | solution.py:58
  181.9 14.4 %stage_four.3 = (bf16[8,256,1280]{2,1,0:T(8,128)(2,1)}, f32[16,1280]{1,0:T(8,128)}, bf16[2,2,2,96,320]{4,3,2,1,0:T(8,128)(2,1)S(1)}, bf16[2,2,2,96,320]{4,3,2,1,...) custom-call(s32[4]{0:T(128)S(1)} %copy-done.6, ...), custom_call_target="tpu_custom_call", output_to_operand_aliasing={{0}: (9, {})} | custom-call | flops 3355443200 | bytes 11796480 | tf_op jit(solution)/shard_map/stage_four/pallas_call | solution.py:995
  199.9 2.1 collective-permute-start.37
  202.0 1.9 collective-permute-start.43
  203.9 3.2 %collective-permute-start.42 = (bf16[80,1120]{1,0:T(8,128)(2,1)S(1)}, bf16[80,1120]{1,0:T(8,128)(2,1)S(1)}, u32[]{:S(2)}, u32[]{:S(2)}) collective-permute-start(bf16[80,1120]{1,0:T(8,128)(2,1)S(1)} %get-tuple-element.191), channel_id=1, source_target_pairs={{0,4},{1,5},{2,6},{3,7},{4,0},{5,1},{6,2},{7,3},{8,12},{9,13},{10,... | collective-permute-start | bytes 537608 | tf_op jit(solution)/shard_map/ppermute | solution.py:58
  207.1 2.0 collective-permute-done.37
  211.2 3.2 %collective-permute-done.38 = bf16[2,96,320]{2,1,0:T(8,128)(2,1)S(1)} collective-permute-done((bf16[2,96,320]{2,1,0:T(8,128)(2,1)S(1)}, bf16[2,96,320]{2,1,0:T(8,128)(2,1)S(1)}, u32[]{:S(2)}, u32[]{:S(2)}) %collective-permute-start.38) | collective-permute-done | bytes 122912 | tf_op jit(solution)/shard_map/ppermute | solution.py:58
  214.5 1.8 collective-permute-start.40
  216.3 3.2 %collective-permute-start.39 = (bf16[96,320]{1,0:T(8,128)(2,1)S(1)}, bf16[96,320]{1,0:T(8,128)(2,1)S(1)}, u32[]{:S(2)}, u32[]{:S(2)}) collective-permute-start(bf16[96,320]{1,0:T(8,128)(2,1)S(1)} %get-tuple-element.195), channel_id=1, source_target_pairs={{0,4},{1,5},{2,6},{3,7},{4,0},{5,1},{6,2},{7,3},{8,12},{9,13},{10,... | collective-permute-start | bytes 184328 | tf_op jit(solution)/shard_map/ppermute | solution.py:58
  221.0 2.6 %collective-permute-done.42.refs_2_ = bf16[80,1120]{1,0:T(8,128)(2,1)S(1)} collective-permute-done((bf16[80,1120]{1,0:T(8,128)(2,1)S(1)}, bf16[80,1120]{1,0:T(8,128)(2,1)S(1)}, u32[]{:S(2)}, u32[]{:S(2)}) %collective-permute-start.42) | collective-permute-done | bytes 179232 | tf_op jit(solution)/shard_map/ppermute | solution.py:58
  (165 shorter events, 39.9 us)
Async XLA Ops:
  2.2 14.0 %collective-permute-start.4 = (bf16[96,320]{1,0:T(8,128)(2,1)}, bf16[96,320]{1,0:T(8,128)(2,1)S(1)}, u32[]{:S(2)}, u32[]{:S(2)}) collective-permute-start(bf16[96,320]{1,0:T(8,128)(2,1)} %pack_first.1), channel_id=1, source_target_pairs={{0,6},{1,7},{2,0},{3,1},{4,2},{5,3},{6,4},{7,5},{8,14},{9,15},{10,... | collective-permute-start | bytes 184328 | tf_op jit(solution)/shard_map/ppermute | solution.py:58
  19.4 16.7 %collective-permute-start.8 = (bf16[80,1120]{1,0:T(8,128)(2,1)}, bf16[80,1120]{1,0:T(8,128)(2,1)S(1)}, u32[]{:S(2)}, u32[]{:S(2)}) collective-permute-start(bf16[80,1120]{1,0:T(8,128)(2,1)} %pack_second.1), channel_id=1, source_target_pairs={{0,4},{1,5},{2,6},{3,7},{4,0},{5,1},{6,2},{7,3},{8,12},{9,13},{10,... | collective-permute-start | bytes 537608 | tf_op jit(solution)/shard_map/ppermute | solution.py:58
  20.5 15.7 %collective-permute-start.7 = (bf16[80,1120]{1,0:T(8,128)(2,1)}, bf16[80,1120]{1,0:T(8,128)(2,1)S(1)}, u32[]{:S(2)}, u32[]{:S(2)}) collective-permute-start(bf16[80,1120]{1,0:T(8,128)(2,1)} %pack_second.1), channel_id=1, source_target_pairs={{0,2},{1,3},{2,4},{3,5},{4,6},{5,7},{6,0},{7,1},{8,10},{9,11},{10,... | collective-permute-start | bytes 537608 | tf_op jit(solution)/shard_map/ppermute | solution.py:58
  22.6 13.7 %collective-permute-start.2 = (bf16[2,2,96,320]{3,2,1,0:T(8,128)(2,1)S(1)}, bf16[2,2,96,320]{3,2,1,0:T(8,128)(2,1)S(1)}, u32[]{:S(2)}, u32[]{:S(2)}) collective-permute-start(bf16[2,2,96,320]{3,2,1,0:T(8,128)(2,1)S(1)} %pad_maximum_fusion.4.refs_0_), channel_id=1, source_target_pairs={{0,16},{1,17},{2,18},{3,19},{4,20},{5,21},{6,22},{7,23},{8,24},{9,... | collective-permute-start | bytes 737288 | tf_op jit(solution)/shard_map/ppermute | solution.py:58
  23.2 13.1 %collective-permute-start.6 = (bf16[2,2,96,320]{3,2,1,0:T(8,128)(2,1)S(1)}, bf16[2,2,96,320]{3,2,1,0:T(8,128)(2,1)S(1)}, u32[]{:S(2)}, u32[]{:S(2)}) collective-permute-start(bf16[2,2,96,320]{3,2,1,0:T(8,128)(2,1)S(1)} %pad_maximum_fusion.5.refs_2_), channel_id=1, source_target_pairs={{0,8},{1,9},{2,10},{3,11},{4,12},{5,13},{6,14},{7,15},{8,0},{9,1},... | collective-permute-start | bytes 737288 | tf_op jit(solution)/shard_map/ppermute | solution.py:58
  46.6 17.9 %collective-permute-start.18 = (bf16[2,2,80,1120]{3,2,1,0:T(8,128)(2,1)S(1)}, bf16[2,2,80,1120]{3,2,1,0:T(8,128)(2,1)S(1)}, u32[]{:S(2)}, u32[]{:S(2)}) collective-permute-start(bf16[2,2,80,1120]{3,2,1,0:T(8,128)(2,1)S(1)} %pad_maximum_fusion.refs_0_), channel_id=1, source_target_pairs={{0,1},{1,0},{2,3},{3,2},{4,5},{5,4},{6,7},{7,6},{8,9},{9,8},{10,11... | collective-permute-start | bytes 2150408 | tf_op jit(solution)/shard_map/ppermute | solution.py:58
  46.8 18.8 %collective-permute-start.16 = (bf16[2,2,80,1120]{3,2,1,0:T(8,128)(2,1)S(1)}, bf16[2,2,80,1120]{3,2,1,0:T(8,128)(2,1)S(1)}, u32[]{:S(2)}, u32[]{:S(2)}) collective-permute-start(bf16[2,2,80,1120]{3,2,1,0:T(8,128)(2,1)S(1)} %pad_maximum_fusion.refs_0_), channel_id=1, source_target_pairs={{0,16},{1,17},{2,18},{3,19},{4,20},{5,21},{6,22},{7,23},{8,24},{9,... | collective-permute-start | bytes 2150408 | tf_op jit(solution)/shard_map/ppermute | solution.py:58
  47.3 18.3 %collective-permute-start.19 = (bf16[2,2,80,1120]{3,2,1,0:T(8,128)(2,1)S(1)}, bf16[2,2,80,1120]{3,2,1,0:T(8,128)(2,1)S(1)}, u32[]{:S(2)}, u32[]{:S(2)}) collective-permute-start(bf16[2,2,80,1120]{3,2,1,0:T(8,128)(2,1)S(1)} %pad_maximum_fusion.1.refs_2_), channel_id=1, source_target_pairs={{0,1},{1,0},{2,3},{3,2},{4,5},{5,4},{6,7},{7,6},{8,9},{9,8},{10,11... | collective-permute-start | bytes 2150408 | tf_op jit(solution)/shard_map/ppermute | solution.py:58
  47.4 18.8 %collective-permute-start.17 = (bf16[2,2,80,1120]{3,2,1,0:T(8,128)(2,1)S(1)}, bf16[2,2,80,1120]{3,2,1,0:T(8,128)(2,1)S(1)}, u32[]{:S(2)}, u32[]{:S(2)}) collective-permute-start(bf16[2,2,80,1120]{3,2,1,0:T(8,128)(2,1)S(1)} %pad_maximum_fusion.1.refs_2_), channel_id=1, source_target_pairs={{0,8},{1,9},{2,10},{3,11},{4,12},{5,13},{6,14},{7,15},{8,0},{9,1},... | collective-permute-start | bytes 2150408 | tf_op jit(solution)/shard_map/ppermute | solution.py:58
  66.7 28.1 %collective-permute-start.20 = (bf16[8,32,640]{2,1,0:T(8,128)(2,1)}, bf16[8,32,640]{2,1,0:T(8,128)(2,1)S(1)}, u32[]{:S(2)}, u32[]{:S(2)}) collective-permute-start(bf16[8,32,640]{2,1,0:T(8,128)(2,1)} %get-tuple-element.127), channel_id=1, source_target_pairs={{0,8},{8,16},{16,24},{1,9},{9,17},{17,25},{2,10},{10,18},{18,26},{... | collective-permute-start | bytes 983048 | tf_op jit(solution)/shard_map/ppermute | solution.py:1016
  69.2 25.7 %collective-permute-start.21 = (bf16[8,32,640]{2,1,0:T(8,128)(2,1)}, bf16[8,32,640]{2,1,0:T(8,128)(2,1)}, u32[]{:S(2)}, u32[]{:S(2)}) collective-permute-start(bf16[8,32,640]{2,1,0:T(8,128)(2,1)} %get-tuple-element.128), channel_id=1, source_target_pairs={{8,0},{16,8},{24,16},{9,1},{17,9},{25,17},{10,2},{18,10},{26,18},{... | collective-permute-start | bytes 983048 | tf_op jit(solution)/shard_map/ppermute | solution.py:1017
  131.9 21.5 %collective-permute-start.24 = (bf16[2,2,2,80,1120]{4,3,2,1,0:T(8,128)(2,1)}, bf16[2,2,2,80,1120]{4,3,2,1,0:T(8,128)(2,1)S(1)}, u32[]{:S(2)}, u32[]{:S(2)}) collective-permute-start(bf16[2,2,2,80,1120]{4,3,2,1,0:T(8,128)(2,1)} %get-tuple-element.140), channel_id=1, source_target_pairs={{0,1},{1,0},{2,3},{3,2},{4,5},{5,4},{6,7},{7,6},{8,9},{9,8},{10,11... | collective-permute-start | bytes 4300808 | tf_op jit(solution)/shard_map/ppermute | solution.py:58
  131.9 22.3 %collective-permute-start.26 = (bf16[8,32,640]{2,1,0:T(8,128)(2,1)}, bf16[8,32,640]{2,1,0:T(8,128)(2,1)S(1)}, u32[]{:S(2)}, u32[]{:S(2)}) collective-permute-start(bf16[8,32,640]{2,1,0:T(8,128)(2,1)} %get-tuple-element.144), channel_id=1, source_target_pairs={{0,8},{8,16},{16,24},{1,9},{9,17},{17,25},{2,10},{10,18},{18,26},{... | collective-permute-start | bytes 983048 | tf_op jit(solution)/shard_map/ppermute | solution.py:1016
  136.9 18.2 %collective-permute-start.27 = (bf16[8,32,640]{2,1,0:T(8,128)(2,1)}, bf16[8,32,640]{2,1,0:T(8,128)(2,1)S(1)}, u32[]{:S(2)}, u32[]{:S(2)}) collective-permute-start(bf16[8,32,640]{2,1,0:T(8,128)(2,1)} %get-tuple-element.145), channel_id=1, source_target_pairs={{8,0},{16,8},{24,16},{9,1},{17,9},{25,17},{10,2},{18,10},{26,18},{... | collective-permute-start | bytes 983048 | tf_op jit(solution)/shard_map/ppermute | solution.py:1017
  138.2 15.6 %collective-permute-start.25 = (bf16[2,2,2,80,1120]{4,3,2,1,0:T(8,128)(2,1)}, bf16[2,2,2,80,1120]{4,3,2,1,0:T(8,128)(2,1)S(1)}, u32[]{:S(2)}, u32[]{:S(2)}) collective-permute-start(bf16[2,2,2,80,1120]{4,3,2,1,0:T(8,128)(2,1)} %get-tuple-element.142), channel_id=1, source_target_pairs={{0,1},{1,0},{2,3},{3,2},{4,5},{5,4},{6,7},{7,6},{8,9},{9,8},{10,11... | collective-permute-start | bytes 4300808 | tf_op jit(solution)/shard_map/ppermute | solution.py:58
  155.2 23.4 %collective-permute-start.29 = (bf16[2,2,80,1120]{3,2,1,0:T(8,128)(2,1)S(1)}, bf16[2,2,80,1120]{3,2,1,0:T(8,128)(2,1)S(1)}, u32[]{:S(2)}, u32[]{:S(2)}) collective-permute-start(bf16[2,2,80,1120]{3,2,1,0:T(8,128)(2,1)S(1)} %slice_bitcast_fusion), channel_id=1, source_target_pairs={{0,8},{1,9},{2,10},{3,11},{4,12},{5,13},{6,14},{7,15},{8,0},{9,1},... | collective-permute-start | bytes 2150408 | tf_op jit(solution)/shard_map/ppermute | solution.py:58
  158.0 20.8 %collective-permute-start.28 = (bf16[2,2,80,1120]{3,2,1,0:T(8,128)(2,1)S(1)}, bf16[2,2,80,1120]{3,2,1,0:T(8,128)(2,1)S(1)}, u32[]{:S(2)}, u32[]{:S(2)}) collective-permute-start(bf16[2,2,80,1120]{3,2,1,0:T(8,128)(2,1)S(1)} %slice_bitcast_fusion.1), channel_id=1, source_target_pairs={{0,16},{1,17},{2,18},{3,19},{4,20},{5,21},{6,22},{7,23},{8,24},{9,... | collective-permute-start | bytes 2150408 | tf_op jit(solution)/shard_map/ppermute | solution.py:58
  179.0 17.3 %collective-permute-start.31 = (bf16[2,80,1120]{2,1,0:T(8,128)(2,1)S(1)}, bf16[2,80,1120]{2,1,0:T(8,128)(2,1)S(1)}, u32[]{:S(2)}, u32[]{:S(2)}) collective-permute-start(bf16[2,80,1120]{2,1,0:T(8,128)(2,1)S(1)} %slice_bitcast_fusion.2), channel_id=1, source_target_pairs={{0,16},{1,17},{2,18},{3,19},{4,20},{5,21},{6,22},{7,23},{8,24},{9,... | collective-permute-start | bytes 1075208 | tf_op jit(solution)/shard_map/ppermute | solution.py:58
  181.8 14.6 %collective-permute-start.30 = (bf16[2,80,1120]{2,1,0:T(8,128)(2,1)S(1)}, bf16[2,80,1120]{2,1,0:T(8,128)(2,1)S(1)}, u32[]{:S(2)}, u32[]{:S(2)}) collective-permute-start(bf16[2,80,1120]{2,1,0:T(8,128)(2,1)S(1)} %slice_bitcast_fusion.3), channel_id=1, source_target_pairs={{0,8},{1,9},{2,10},{3,11},{4,12},{5,13},{6,14},{7,15},{8,0},{9,1},... | collective-permute-start | bytes 1075208 | tf_op jit(solution)/shard_map/ppermute | solution.py:58
  199.6 19.9 %collective-permute-start.41 = (bf16[80,1120]{1,0:T(8,128)(2,1)S(1)}, bf16[80,1120]{1,0:T(8,128)(2,1)S(1)}, u32[]{:S(2)}, u32[]{:S(2)}) collective-permute-start(bf16[80,1120]{1,0:T(8,128)(2,1)S(1)} %get-tuple-element.192), channel_id=1, source_target_pairs={{0,6},{1,7},{2,0},{3,1},{4,2},{5,3},{6,4},{7,5},{8,14},{9,15},{10,... | collective-permute-start | bytes 537608 | tf_op jit(solution)/shard_map/ppermute | solution.py:58
  199.9 9.2 %collective-permute-start.37 = (bf16[2,2,96,320]{3,2,1,0:T(8,128)(2,1)S(1)}, bf16[2,2,96,320]{3,2,1,0:T(8,128)(2,1)S(1)}, u32[]{:S(2)}, u32[]{:S(2)}) collective-permute-start(bf16[2,2,96,320]{3,2,1,0:T(8,128)(2,1)S(1)} %slice_bitcast_fusion.4), channel_id=1, source_target_pairs={{0,8},{1,9},{2,10},{3,11},{4,12},{5,13},{6,14},{7,15},{8,0},{9,1},... | collective-permute-start | bytes 737288 | tf_op jit(solution)/shard_map/ppermute | solution.py:58
  202.0 19.0 %collective-permute-start.43 = (bf16[80,1120]{1,0:T(8,128)(2,1)S(1)}, bf16[80,1120]{1,0:T(8,128)(2,1)S(1)}, u32[]{:S(2)}, u32[]{:S(2)}) collective-permute-start(bf16[80,1120]{1,0:T(8,128)(2,1)S(1)} %get-tuple-element.190), channel_id=1, source_target_pairs={{0,2},{1,3},{2,4},{3,5},{4,6},{5,7},{6,0},{7,1},{8,10},{9,11},{10,... | collective-permute-start | bytes 537608 | tf_op jit(solution)/shard_map/ppermute | solution.py:58
  203.9 19.6 %collective-permute-start.42 = (bf16[80,1120]{1,0:T(8,128)(2,1)S(1)}, bf16[80,1120]{1,0:T(8,128)(2,1)S(1)}, u32[]{:S(2)}, u32[]{:S(2)}) collective-permute-start(bf16[80,1120]{1,0:T(8,128)(2,1)S(1)} %get-tuple-element.191), channel_id=1, source_target_pairs={{0,4},{1,5},{2,6},{3,7},{4,0},{5,1},{6,2},{7,3},{8,12},{9,13},{10,... | collective-permute-start | bytes 537608 | tf_op jit(solution)/shard_map/ppermute | solution.py:58
  214.5 10.1 %collective-permute-start.40 = (bf16[96,320]{1,0:T(8,128)(2,1)S(1)}, bf16[96,320]{1,0:T(8,128)(2,1)S(1)}, u32[]{:S(2)}, u32[]{:S(2)}) collective-permute-start(bf16[96,320]{1,0:T(8,128)(2,1)S(1)} %get-tuple-element.194), channel_id=1, source_target_pairs={{0,2},{1,3},{2,4},{3,5},{4,6},{5,7},{6,0},{7,1},{8,10},{9,11},{10,... | collective-permute-start | bytes 184328 | tf_op jit(solution)/shard_map/ppermute | solution.py:58
  (48 other events, 367.6 us)
